TPU v7x, 128 devices: a whole 4x4x4 slice. The times are simulated.
128 devices in a mesh: box: 64 (over y, x, z), dir: 2 (over core).
Axes of the slice: x: 4, y: 4, z: 4, core: 2. Of those that a mesh axis runs over, the one named last changes fastest.
Arguments:
- sources: bfloat16 [512, 2, 64, 512], P('box'), may hold values from -6 to 6
- near_blocks: bfloat16 [512, 3, 2, 512, 512], P('box', None, None, 'dir'), may hold values from -0.109375 to 0.109375
- near_src: int32 [512, 3], P('box'), may hold values from 0 to 511, as said below
- radiation: bfloat16 [512, 2, 512, 1024], P('box', None, None, 'dir'), may hold values from -0.1875 to 0.1875
- il0_src: int32 [512, 16], P('box'), may hold values from 0 to 511, as said below
- il0_rel: int32 [512, 16], P('box'), may hold values from 0 to 315
- il0_count: int32 [512], P('box'), may hold values from 1 to 16, as said below
- trans0: bfloat16 [316, 2, 1024], P(None, None, 'dir'), may hold values from -1 to 1
- phi_interp1: bfloat16 [64, 128], replicated, may hold values from -0.75 to 0.75
- theta_interp1: bfloat16 [32, 16], replicated, may hold values from -1.5 to 1.5
- shift1: bfloat16 [8, 2, 4096], replicated, may hold values from -1.5 to 1.5
- phi_interp2: bfloat16 [128, 256], replicated, may hold values from -0.5 to 0.5
- theta_interp2: bfloat16 [64, 32], replicated, may hold values from -1 to 1
- shift2: bfloat16 [8, 2, 16384], replicated, may hold values from -1.5 to 1.5
- il2_src: int32 [8, 4], replicated, may hold values from 0 to 7
- il2_rel: int32 [8, 4], replicated, may hold values from 0 to 315
- trans2: bfloat16 [316, 2, 64, 256], P(None, None, 'box', 'dir'), may hold values from -2 to 2
Outputs:
- near_field: float32 [512, 2, 64, 512], P('box', None, None, 'dir')
- leaf_incoming: float32 [512, 2, 64, 1024], P('box', None, None, 'dir')
- upper_incoming: float32 [8, 2, 64, 64, 256], P(None, None, None, 'box', 'dir')
Inputs may be any that keep to these rules, and one draw needn't show every extreme that they name: `near_src`: every entry is a leaf box whose owner index (box // 8) differs from the owner index of the row's own box by at most one; the first entry of row b is b itself. `il0_src`: every entry is a leaf box whose owner index (box // 8) differs from the owner index of the row's own box by at most one. `il0_count`: among the 8 boxes of every owner, one has 16 valid entries.
All inputs are finite; a program needn't handle non-finite values.
Results may differ from a plain program's by a relative error of at most 0.012.
Values may be sent and summed in bfloat16 or wider, within the bound.
No kernel may reach another device: no remote copies, remote signals or barrier semaphores. Data moves between devices by JAX's collectives and lax.ppermute only.
A program may use at most 192 MiB of HBM per device.

v0:
```python
import jax
import jax.numpy as jnp
from jax import lax
from jax.sharding import PartitionSpec as P


def padded(cells, sides, width):
    for axis, dim in sides:
        count = lax.axis_size(axis)
        ends = count - 1
        head = lax.slice_in_dim(cells, 0, width, axis=dim)
        tail = lax.slice_in_dim(cells, cells.shape[dim] - width, cells.shape[dim], axis=dim)
        cells = jnp.concatenate(
            [
                lax.ppermute(tail, axis, [(i, (i + 1) % count) for i in range(ends)]),
                cells,
                lax.ppermute(head, axis, [((i + 1) % count, i) for i in range(ends)]),
            ],
            axis=dim,
        )
    return cells


def pair_up(products):
    real_part = products[:, 0, 0] - products[:, 1, 1]
    imag_part = products[:, 0, 1] + products[:, 1, 0]
    return jnp.stack([real_part, imag_part], axis=1)


def translate(fetched, operators, weights):
    op_real = (operators[:, :, 0] * weights[:, :, None])[:, :, None, :]
    op_imag = (operators[:, :, 1] * weights[:, :, None])[:, :, None, :]
    real_part = jnp.sum(op_real * fetched[:, :, 0] - op_imag * fetched[:, :, 1], axis=1)
    imag_part = jnp.sum(op_real * fetched[:, :, 1] + op_imag * fetched[:, :, 0], axis=1)
    return jnp.stack([real_part, imag_part], axis=1)


def shifted_sum(values, factors):
    factor_real = factors[:, 0][:, None, :]
    factor_imag = factors[:, 1][:, None, :]
    real_part = jnp.sum(values[:, 0] * factor_real - values[:, 1] * factor_imag, axis=0)
    imag_part = jnp.sum(values[:, 0] * factor_imag + values[:, 1] * factor_real, axis=0)
    return jnp.stack([real_part, imag_part], axis=0)


def scale_pattern(values, factors):
    factor_real = factors[0][None, :]
    factor_imag = factors[1][None, :]
    real_part = values[0] * factor_real - values[1] * factor_imag
    imag_part = values[0] * factor_imag + values[1] * factor_real
    return jnp.stack([real_part, imag_part], axis=0)


def local(
    sources,
    near_blocks,
    near_src,
    radiation,
    il0_src,
    il0_rel,
    il0_count,
    trans0,
    phi_interp1,
    theta_interp1,
    shift1,
    phi_interp2,
    theta_interp2,
    shift2,
    il2_src,
    il2_rel,
    trans2,
):
    box_count = sources.shape[0]
    headings = sources.shape[2]
    dir_count = lax.axis_size("dir")
    box_total = lax.axis_size("box")
    dir_index = lax.axis_index("dir")
    box_index = lax.axis_index("box")
    first_box = (box_index - 1) * box_count
    widened = padded(sources, (("box", 0),), box_count)
    picked = widened[near_src - first_box]
    near_field = pair_up(
        jnp.einsum("bjcqp,bjerp->bcerq", near_blocks, picked, preferred_element_type=jnp.float32)
    )
    leaf_out = pair_up(
        jnp.einsum("berp,bcpk->bcerk", sources, radiation, preferred_element_type=jnp.float32)
    ).astype(jnp.bfloat16)
    leaf_wide = padded(leaf_out, (("box", 0),), box_count)
    fetched = leaf_wide[il0_src - first_box].astype(jnp.float32)
    operators = trans0[il0_rel].astype(jnp.float32)
    weights = (jnp.arange(il0_src.shape[1], dtype=jnp.int32)[None, :] < il0_count[:, None]).astype(
        jnp.float32
    )
    leaf_incoming = translate(fetched, operators, weights)
    theta_rows = theta_interp1.shape[0]
    theta_cols = theta_interp1.shape[1]
    phi_cols = phi_interp1.shape[0]
    full = lax.all_gather(leaf_out, "dir", axis=3, tiled=True)
    shaped = full.reshape(box_count, 2, headings, theta_cols, phi_cols)
    along_phi = jnp.einsum(
        "bcrtp,pq->bcrtq", shaped, phi_interp1, preferred_element_type=jnp.float32
    ).astype(jnp.bfloat16)
    half_rows = theta_rows // dir_count
    rows = lax.dynamic_slice_in_dim(theta_interp1, dir_index * half_rows, half_rows, 0)
    along_theta = jnp.einsum("st,bcrtq->bcrsq", rows, along_phi, preferred_element_type=jnp.float32)
    along_theta = along_theta.reshape(box_count, 2, headings, -1)
    span = along_theta.shape[3]
    factors = lax.dynamic_slice_in_dim(shift1, dir_index * span, span, 2).astype(jnp.float32)
    parent = shifted_sum(along_theta, factors).astype(jnp.bfloat16)
    half_one = theta_interp2.shape[1] // dir_count
    phi_one = phi_interp2.shape[0]
    theta_two = theta_interp2.shape[0]
    phi_two = phi_interp2.shape[1]
    level_boxes = box_total // 8
    parent_grid = parent.reshape(2, headings, half_one, phi_one)
    upper_phi = jnp.einsum(
        "crtp,pq->crtq", parent_grid, phi_interp2, preferred_element_type=jnp.float32
    ).astype(jnp.bfloat16)
    upper_columns = lax.dynamic_slice_in_dim(theta_interp2, dir_index * half_one, half_one, 1)
    upper_theta = jnp.einsum(
        "st,crtq->crsq", upper_columns, upper_phi, preferred_element_type=jnp.float32
    )
    upper_theta = upper_theta.reshape(2, headings, -1)
    octant = lax.dynamic_index_in_dim(shift2, box_index % 8, 0, keepdims=False).astype(jnp.float32)
    halved = lax.psum_scatter(
        scale_pattern(upper_theta, octant)
        .reshape(1, 2, headings, theta_two, phi_two)
        .astype(jnp.bfloat16),
        "dir",
        scatter_dimension=4,
        tiled=True,
    ).astype(jnp.float32)
    received = lax.all_to_all(
        halved.astype(jnp.bfloat16), "box", split_axis=3, concat_axis=0, tiled=True
    ).astype(halved.dtype)
    level_two = jnp.sum(
        received.reshape(level_boxes, 8, 2, headings, received.shape[3], received.shape[4]), axis=1
    )
    row_count = level_two.shape[3]
    col_count = level_two.shape[4]
    flat_two = level_two.reshape(level_boxes, 2, headings, row_count * col_count)
    upper_fetched = flat_two[il2_src]
    upper_operators = (
        trans2[il2_rel]
        .reshape(il2_src.shape[0], il2_src.shape[1], 2, row_count * col_count)
        .astype(jnp.float32)
    )
    upper_incoming = translate(upper_fetched, upper_operators, jnp.ones(il2_src.shape, jnp.float32))
    upper_incoming = upper_incoming.reshape(level_boxes, 2, headings, row_count, col_count)
    return (near_field, leaf_incoming, upper_incoming)


def solution(mesh):
    placed = (
        P("box", None, None, None),
        P("box", None, None, "dir", None),
        P("box", None),
        P("box", None, None, "dir"),
        P("box", None),
        P("box", None),
        P("box"),
        P(None, None, "dir"),
        P(),
        P(),
        P(),
        P(),
        P(),
        P(),
        P(),
        P(),
        P(None, None, "box", "dir"),
    )
    return jax.shard_map(
        local,
        mesh=mesh,
        in_specs=placed,
        out_specs=(
            P("box", None, None, "dir"),
            P("box", None, None, "dir"),
            P(None, None, None, "box", "dir"),
        ),
        check_vma=False,
    )
```

profile of v0, /device:TPU:1, one launch (start us, length us, event | category | flops | bytes accessed | tf_op | source)
XLA Modules:
  0.0 253.3 jit_solution(18429624648020062764)
XLA Ops:
  7.2 0.0 all-gather.2.cloned.1.call-start
  7.2 4.9 %fusion.18 = f32[8,2,2,64,512]{4,3,2,1,0:T(8,128)S(1)} fusion(bf16[8,2,512,512]{3,2,1,0:T(8,128)(2,1)} %param.20, bf16[8,2,64,512]{3,2,1,0:T(8,128)(2,1)} %param.17), kind=kOutput, calls=%fused_computation.29 | convolution fusion | flops 1073741824 | bytes 13631488 | tf_op jit(solution)/shard_map/berp,bcpk->bcerk/dot_general | solution.py:86
  12.2 0.2 fusion.32
  12.4 0.2 fusion.33
  12.5 1.1 pad_maximum_fusion.5
  13.6 0.0 reduce-scatter.4.cloned.1.call-start
  13.7 0.9 dynamic-slice_convert_fusion
  14.6 0.3 slice_reduce_fusion.1
  15.0 0.1 constant_dynamic-slice_fusion
  15.1 15.6 %all-gather.2.cloned.1.call-done = bf16[8,2,64,1024]{3,2,0,1:T(8,128)(2,1)} async-done(((bf16[8,2,64,512]{3,2,0,1:T(8,128)(2,1)}), bf16[8,2,64,1024]{3,2,0,1:T(8,128)(2,1)}) %all-gather.2.cloned.1.call-update) | async-done | bytes 2097168 | tf_op jit(solution)/shard_map/all_gather | solution.py:98
  30.7 6.4 %reshape.241 = bf16[8,2,64,16,64]{4,3,2,0,1:T(8,128)(2,1)} reshape(bf16[8,2,64,1024]{3,2,0,1:T(8,128)(2,1)} %all-gather.2.cloned.1.call-done) | data formatting | bytes 4194304 | tf_op jit(solution)/shard_map/reshape | solution.py:99
  37.1 6.3 %fusion.12 = f32[8,2,64,16,128]{4,3,2,1,0:T(8,128)} fusion(bf16[8,2,64,16,64]{4,3,2,0,1:T(8,128)(2,1)} %reshape.241, bf16[64,128]{1,0:T(8,128)(2,1)S(1)} %copy-done.7, bf16[32,16]{0,1:T(8,128)(2,1)S(1)} %copy-done.8, s32[]{:T(128)S(6)} %select_n.37), kind=kOutput, calls=%fused_computation.24 | convolution fusion | flops 337641472 | bytes 10503172 | tf_op jit(solution)/shard_map/st,bcrtq->bcrsq/dot_general | solution.py:105
  43.4 9.2 %reshape.242 = f32[8,2,64,2048]{3,2,1,0:T(8,128)} reshape(f32[8,2,64,16,128]{4,3,2,1,0:T(8,128)} %fusion.12) | data formatting | bytes 16777216 | tf_op jit(solution)/shard_map/reshape | solution.py:106
  52.6 4.8 %subtract_reduce_fusion.1 = (bf16[64,2048]{1,0:T(8,128)(2,1)S(1)}, bf16[64,2048]{1,0:T(8,128)(2,1)S(1)}) fusion(f32[8,2,64,2048]{3,2,1,0:T(8,128)} %reshape.242, f32[8,2048]{1,0:T(8,128)S(1)} %get-tuple-element.25, f32[8,2048]{1,0:T(8,128)S(1)} %get-tuple-element.24), kind=kLoop, calls=%fused_computation.21 | loop fusion | flops 8126464 | bytes 9043968 | tf_op jit(solution)/shard_map/reduce_sum | solution.py:41
  57.6 4.9 %convolution_bitcast_fusion = f32[2,64,64,256]{3,2,1,0:T(8,128)} fusion(bf16[1,64,16,128]{3,2,1,0:T(8,128)(2,1)S(1)} %bitcast.191, bf16[1,64,16,128]{3,2,1,0:T(8,128)(2,1)S(1)} %bitcast.190, bf16[128,256]{1,0:T(8,128)(2,1)S(1)} %copy-done.5, bf16[64,32]{0,1:T(8,128)(2,1)S(1)} %copy-done.11, s32[]{:T(128)S(6)} %select_n.37), kind=kOutput, calls=%fused_computation.25 | convolution fusion | flops 202113024 | bytes 8982532 | tf_op jit(solution)/shard_map/st,crtq->crsq/dot_general | solution.py:120
  62.4 4.9 %fusion.21 = (bf16[1,1,64,64,256]{4,3,2,1,0:T(8,128)(2,1)S(1)}, bf16[1,1,64,64,256]{4,3,2,1,0:T(8,128)(2,1)S(1)}) fusion(f32[2,64,64,256]{3,2,1,0:T(8,128)} %convolution_bitcast_fusion, f32[64,256]{1,0:T(8,128)S(1)} %mul.189, f32[64,256]{1,0:T(8,128)S(1)} %mul.186), kind=kLoop, calls=%fused_computation.30 | loop fusion | flops 8388608 | bytes 12713984 | tf_op jit(solution)/shard_map/stack | solution.py:51
  67.3 2.3 pad_maximum_fusion
  69.6 13.0 %copy.80 = bf16[1,2,64,64,256]{3,2,1,0,4:T(8,128)(2,1)} copy(bf16[1,2,64,64,256]{4,3,2,1,0:T(8,128)(2,1)} %pad_maximum_fusion) | data formatting | bytes 8388608
  82.6 12.0 %reshape.313 = bf16[256,8192]{1,0:T(8,128)(2,1)} reshape(bf16[256,1,2,64,64]{4,3,2,1,0:T(8,128)(2,1)} %bitcast.181) | data formatting | bytes 8388608
  94.7 0.0 reduce-scatter.4.cloned.1.call-update
  94.7 1.1 copy-done.2
  95.9 4.4 %collective-permute-start.2 = (bf16[8,2,64,512]{3,2,0,1:T(8,128)(2,1)S(1)}, bf16[8,2,64,512]{3,2,0,1:T(8,128)(2,1)}, u32[]{:S(2)}, u32[]{:S(2)}) collective-permute-start(bf16[8,2,64,512]{3,2,0,1:T(8,128)(2,1)S(1)} %copy-done.2), channel_id=1, source_target_pairs={{0,2},{2,4},{4,6},{6,8},{8,10},{10,12},{12,14},{14,16},{16,18},{18... | collective-permute-start | bytes 3145736 | tf_op jit(solution)/shard_map/ppermute | solution.py:15
  100.3 1.3 collective-permute-start.3
  101.6 5.0 %collective-permute-start = (bf16[8,2,64,512]{3,2,1,0:T(8,128)(2,1)}, bf16[8,2,64,512]{3,2,1,0:T(8,128)(2,1)}, u32[]{:S(2)}, u32[]{:S(2)}) collective-permute-start(bf16[8,2,64,512]{3,2,1,0:T(8,128)(2,1)} %param.17), channel_id=1, source_target_pairs={{0,2},{2,4},{4,6},{6,8},{8,10},{10,12},{12,14},{14,16},{16,18},{18... | collective-permute-start | bytes 3145736 | tf_op jit(solution)/shard_map/ppermute | solution.py:15
  106.6 1.3 collective-permute-start.1
  107.9 0.1 copy.63
  108.0 0.1 reshape.283
  108.1 0.1 copy.56
  108.2 0.1 reshape.275
  108.2 0.1 reshape.265
  108.3 0.1 reshape.257
  108.4 0.1 copy.48
  108.5 0.1 reshape.249
  108.7 0.1 fusion.51
  108.7 1.1 gather_fusion.1
  109.9 0.2 convert.34
  110.1 1.5 gather_fusion.3
  111.6 0.4 slice_multiply_fusion.1
  112.1 9.4 %collective-permute-done.2 = bf16[8,2,64,512]{3,2,0,1:T(8,128)(2,1)} collective-permute-done((bf16[8,2,64,512]{3,2,0,1:T(8,128)(2,1)S(1)}, bf16[8,2,64,512]{3,2,0,1:T(8,128)(2,1)}, u32[]{:S(2)}, u32[]{:S(2)}) %collective-permute-start.2) | collective-permute-done | bytes 1048608 | tf_op jit(solution)/shard_map/ppermute | solution.py:15
  121.5 5.1 %collective-permute-done.3 = bf16[8,2,64,512]{3,2,0,1:T(8,128)(2,1)} collective-permute-done((bf16[8,2,64,512]{3,2,0,1:T(8,128)(2,1)S(1)}, bf16[8,2,64,512]{3,2,0,1:T(8,128)(2,1)}, u32[]{:S(2)}, u32[]{:S(2)}) %collective-permute-start.3) | collective-permute-done | bytes 1048608 | tf_op jit(solution)/shard_map/ppermute | solution.py:17
  126.6 3.0 %pad_maximum_fusion.2 = bf16[24,2,64,512]{3,2,0,1:T(8,128)(2,1)} fusion(bf16[8,2,64,512]{3,2,0,1:T(8,128)(2,1)} %collective-permute-done.3, bf16[8,1,64,512]{3,2,0,1:T(8,128)(2,1)S(1)} %fusion.33, bf16[8,1,64,512]{3,2,0,1:T(8,128)(2,1)S(1)} %fusion.32, bf16[8,2,64,512]{3,2,0,1:T(8,128)(2,1)} %collective-permute-done.2), kind=kLoop, calls=%fused_computation.27 | loop fusion | flops 4718592 | bytes 6291456 | tf_op jit(solution)/shard_map/concatenate | solution.py:13
  129.6 10.3 %gather_fusion.2 = bf16[128,2,64,512]{3,2,1,0:T(8,128)(2,1)} fusion(bf16[24,2,64,512]{3,2,0,1:T(8,128)(2,1)} %pad_maximum_fusion.2, s32[1024]{0:T(1024)S(1)} %pad_clamp_fusion.2), kind=kCustom, calls=%fused_computation.2 | custom fusion | bytes 33554944 | tf_op jit(solution)/shard_map/gather | solution.py:89
  139.9 4.2 %collective-permute-done = bf16[8,2,64,512]{3,2,1,0:T(8,128)(2,1)} collective-permute-done((bf16[8,2,64,512]{3,2,1,0:T(8,128)(2,1)}, bf16[8,2,64,512]{3,2,1,0:T(8,128)(2,1)}, u32[]{:S(2)}, u32[]{:S(2)}) %collective-permute-start) | collective-permute-done | bytes 1048608 | tf_op jit(solution)/shard_map/ppermute | solution.py:15
  144.1 5.0 %collective-permute-done.1 = bf16[8,2,64,512]{3,2,1,0:T(8,128)(2,1)} collective-permute-done((bf16[8,2,64,512]{3,2,1,0:T(8,128)(2,1)}, bf16[8,2,64,512]{3,2,1,0:T(8,128)(2,1)}, u32[]{:S(2)}, u32[]{:S(2)}) %collective-permute-start.1) | collective-permute-done | bytes 1048608 | tf_op jit(solution)/shard_map/ppermute | solution.py:17
  149.0 3.0 %pad_maximum_fusion.1 = bf16[24,2,64,512]{3,2,1,0:T(8,128)(2,1)} fusion(bf16[8,2,64,512]{3,2,1,0:T(8,128)(2,1)} %collective-permute-done.1, bf16[8,2,64,512]{3,2,1,0:T(8,128)(2,1)S(1)} %copy-done.3, bf16[8,2,64,512]{3,2,1,0:T(8,128)(2,1)} %collective-permute-done), kind=kLoop, calls=%fused_computation.26 | loop fusion | flops 3145728 | bytes 6291456 | tf_op jit(solution)/shard_map/concatenate | solution.py:13
  152.1 4.4 %gather_fusion = bf16[24,2,64,512]{3,2,1,0:T(8,128)(2,1)} fusion(bf16[24,2,64,512]{3,2,1,0:T(8,128)(2,1)} %pad_maximum_fusion.1, s32[1024]{0:T(1024)S(1)} %pad_clamp_fusion.4), kind=kCustom, calls=%fused_computation | custom fusion | bytes 6291552 | tf_op jit(solution)/shard_map/gather | solution.py:81
  156.5 8.1 %fusion.23 = f32[8,2,2,64,256]{4,3,1,2,0:T(8,128)S(1)} fusion(bf16[8,3,2,64,512,1]{4,3,2,1,0,5:T(8,128)(2,1)} %bitcast.187, bf16[8,3,2,256,512]{4,3,2,1,0:T(8,128)(2,1)} %param.18), kind=kOutput, calls=%fused_computation.34 | convolution fusion | flops 1610612736 | bytes 17825792 | tf_op jit(solution)/shard_map/bjcqp,bjerp->bcerq/dot_general | solution.py:83
  164.6 1.3 copy-done.4
  165.9 0.1 fusion.34
  166.0 18.8 %bitcast_convert_fusion.1 = f32[8,16,2,64,512]{4,3,2,1,0:T(8,128)} fusion(bf16[128,2,64,512]{3,2,1,0:T(8,128)(2,1)} %gather_fusion.2), kind=kLoop, calls=%fused_computation.95 | loop fusion | flops 8388608 | bytes 50331648 | tf_op jit(solution)/shard_map/convert_element_type | solution.py:89
  184.8 6.9 %reshape.314 = bf16[128,1,2,64,64]{4,3,2,1,0:T(8,128)(2,1)} reshape(bf16[128,8192]{1,0:T(8,128)(2,1)} %reduce-scatter.4.cloned.1.call-done) | data formatting | bytes 4194304
  191.7 8.5 %copy.61 = bf16[1,2,64,64,128]{4,2,1,0,3:T(8,128)(2,1)} copy(bf16[1,2,64,64,128]{3,2,1,0,4:T(8,128)(2,1)} %bitcast.183) | data formatting | bytes 4194304 | tf_op jit(solution)/shard_map/reduce_scatter | solution.py:125
  200.2 12.1 %all-to-all-start = ((bf16[1,2,64,64,128]{4,2,1,0,3:T(8,128)(2,1)}), bf16[1,2,64,64,128]{4,2,1,0,3:T(8,128)(2,1)S(1)}, u32[]{:S(2)}, u32[]{:S(2)}) async-start(bf16[1,2,64,64,128]{4,2,1,0,3:T(8,128)(2,1)} %copy.61), calls=%async_computation | async-start | bytes 4194304 | tf_op jit(solution)/shard_map/all_to_all | solution.py:133
  212.3 1.3 fusion.36
  213.6 0.1 pad_maximum_fusion.4
  213.7 1.1 copy.66
  214.8 13.0 %subtract_reduce_fusion = (f32[8,64,512]{2,1,0:T(8,128)S(1)}, f32[8,64,512]{2,1,0:T(8,128)S(1)}) fusion(f32[8,16,2,64,512]{4,3,2,1,0:T(8,128)} %bitcast_convert_fusion.1, f32[8,16,512]{2,1,0:T(8,128)S(1)} %get-tuple-element.28, f32[8,16,512]{2,1,0:T(8,128)S(1)} %get-tuple-element.29), kind=kLoop, calls=%fused_computation.8 | loop fusion | flops 33030144 | bytes 36175872 | tf_op jit(solution)/shard_map/reduce_sum | solution.py:33
  227.8 1.5 pad_maximum_fusion.3
  229.3 10.2 %all-to-all-done = bf16[1,2,64,64,128]{4,2,1,0,3:T(8,128)(2,1)S(1)} async-done(((bf16[1,2,64,64,128]{4,2,1,0,3:T(8,128)(2,1)}), bf16[1,2,64,64,128]{4,2,1,0,3:T(8,128)(2,1)S(1)}, u32[]{:S(2)}, u32[]{:S(2)}) %all-to-all-start) | async-done | bytes 2097184 | tf_op jit(solution)/shard_map/all_to_all | solution.py:133
  239.4 2.4 bitcast_convert_fusion
  241.8 2.7 %reduce_sum.67 = f32[8,2,64,128]{3,2,1,0:T(8,128)S(1)} reduce(f32[8,8,2,64,128]{4,3,2,1,0:T(8,128)} %bitcast.182, f32[]{:T(128)} %constant.20.clone.1), dimensions={1}, to_apply=%region_5.6 | reduce | flops 917504 | bytes 4718596 | tf_op jit(solution)/shard_map/reduce_sum | solution.py:136
  244.5 0.7 gather_fusion.4
  245.2 0.3 subtract_reduce_fusion.2
  245.6 0.8 pad_maximum_fusion.6
  (50 shorter events, 0.4 us)
Async XLA Ops:
  7.2 101.6 %copy-start = (bf16[316,2,512]{2,1,0:T(2,128)(2,1)S(1)}, bf16[316,2,512]{2,1,0:T(2,128)(2,1)}, u32[]{:S(2)}) copy-start(bf16[316,2,512]{2,1,0:T(2,128)(2,1)} %param.24) | copy-start | bytes 1941508
  7.2 23.5 %all-gather.2.cloned.1.call-start = ((), (), s32[]{:S(2)}) async-start(), calls=%async_computation.2 | async-start | bytes 3145728 | tf_op jit(solution)/shard_map/all_gather | solution.py:98
  12.2 2.8 %copy-start.6 = (bf16[8,2,4096]{2,1,0:T(2,128)(2,1)S(1)}, bf16[8,2,4096]{2,1,0:T(2,128)(2,1)}, u32[]{:S(2)}) copy-start(bf16[8,2,4096]{2,1,0:T(2,128)(2,1)} %param.27) | copy-start | bytes 393220
  13.6 23.5 %copy-start.7 = (bf16[64,128]{1,0:T(8,128)(2,1)S(1)}, bf16[64,128]{1,0:T(8,128)(2,1)}, u32[]{:S(2)}) copy-start(bf16[64,128]{1,0:T(8,128)(2,1)} %param.25) | copy-start | bytes 49156
  13.6 23.5 %copy-start.8 = (bf16[32,16]{0,1:T(8,128)(2,1)S(1)}, bf16[32,16]{0,1:T(8,128)(2,1)}, u32[]{:S(2)}) copy-start(bf16[32,16]{0,1:T(8,128)(2,1)} %param.26) | copy-start | bytes 3076
  13.6 171.1 %reduce-scatter.4.cloned.1.call-start = ((), (), s32[]{:S(2)}) async-start(), calls=%async_computation.3 | async-start | bytes 6291456
  52.6 4.9 %copy-start.5 = (bf16[128,256]{1,0:T(8,128)(2,1)S(1)}, bf16[128,256]{1,0:T(8,128)(2,1)}, u32[]{:S(2)}) copy-start(bf16[128,256]{1,0:T(8,128)(2,1)} %param.28) | copy-start | bytes 196612
  52.6 4.9 %copy-start.11 = (bf16[64,32]{0,1:T(8,128)(2,1)S(1)}, bf16[64,32]{0,1:T(8,128)(2,1)}, u32[]{:S(2)}) copy-start(bf16[64,32]{0,1:T(8,128)(2,1)} %param.29) | copy-start | bytes 12292
  94.7 1.2 copy-start.2
  94.7 13.2 %copy-start.12 = (s32[8,4]{0,1:T(4,128)S(1)}, s32[8,4]{0,1:T(4,128)}, u32[]{:S(2)}) copy-start(s32[8,4]{0,1:T(4,128)} %param.31) | copy-start | bytes 388
  94.7 13.4 %copy-start.13 = (s32[8,4]{0,1:T(4,128)S(1)}, s32[8,4]{0,1:T(4,128)}, u32[]{:S(2)}) copy-start(s32[8,4]{0,1:T(4,128)} %param.32) | copy-start | bytes 388
  94.7 13.6 %copy-start.9 = (s32[8,16]{1,0:T(8,128)S(1)}, s32[8,16]{1,0:T(8,128)}, u32[]{:S(2)}) copy-start(s32[8,16]{1,0:T(8,128)} %param.21) | copy-start | bytes 1540
  94.7 13.7 %copy-start.10 = (s32[8,16]{1,0:T(8,128)S(1)}, s32[8,16]{1,0:T(8,128)}, u32[]{:S(2)}) copy-start(s32[8,16]{1,0:T(8,128)} %param.22) | copy-start | bytes 1540
  94.7 13.7 %copy-start.14 = (s32[8,3]{0,1:T(4,128)S(1)}, s32[8,3]{0,1:T(4,128)}, u32[]{:S(2)}) copy-start(s32[8,3]{0,1:T(4,128)} %param.19) | copy-start | bytes 292
  94.7 14.0 %copy-start.15 = (s32[8]{0:T(128)S(1)}, s32[8]{0:T(128)}, u32[]{:S(2)}) copy-start(s32[8]{0:T(128)} %param.23) | copy-start | bytes 100
  95.9 25.6 %collective-permute-start.2 = (bf16[8,2,64,512]{3,2,0,1:T(8,128)(2,1)S(1)}, bf16[8,2,64,512]{3,2,0,1:T(8,128)(2,1)}, u32[]{:S(2)}, u32[]{:S(2)}) collective-permute-start(bf16[8,2,64,512]{3,2,0,1:T(8,128)(2,1)S(1)} %copy-done.2), channel_id=1, source_target_pairs={{0,2},{2,4},{4,6},{6,8},{8,10},{10,12},{12,14},{14,16},{16,18},{18... | collective-permute-start | bytes 3145736 | tf_op jit(solution)/shard_map/ppermute | solution.py:15
  100.3 26.2 %collective-permute-start.3 = (bf16[8,2,64,512]{3,2,0,1:T(8,128)(2,1)S(1)}, bf16[8,2,64,512]{3,2,0,1:T(8,128)(2,1)}, u32[]{:S(2)}, u32[]{:S(2)}) collective-permute-start(bf16[8,2,64,512]{3,2,0,1:T(8,128)(2,1)S(1)} %copy-done.2), channel_id=1, source_target_pairs={{2,0},{4,2},{6,4},{8,6},{10,8},{12,10},{14,12},{16,14},{18,16},{20... | collective-permute-start | bytes 3145736 | tf_op jit(solution)/shard_map/ppermute | solution.py:17
  101.6 42.4 %collective-permute-start = (bf16[8,2,64,512]{3,2,1,0:T(8,128)(2,1)}, bf16[8,2,64,512]{3,2,1,0:T(8,128)(2,1)}, u32[]{:S(2)}, u32[]{:S(2)}) collective-permute-start(bf16[8,2,64,512]{3,2,1,0:T(8,128)(2,1)} %param.17), channel_id=1, source_target_pairs={{0,2},{2,4},{4,6},{6,8},{8,10},{10,12},{12,14},{14,16},{16,18},{18... | collective-permute-start | bytes 3145736 | tf_op jit(solution)/shard_map/ppermute | solution.py:15
  106.6 42.4 %collective-permute-start.1 = (bf16[8,2,64,512]{3,2,1,0:T(8,128)(2,1)}, bf16[8,2,64,512]{3,2,1,0:T(8,128)(2,1)}, u32[]{:S(2)}, u32[]{:S(2)}) collective-permute-start(bf16[8,2,64,512]{3,2,1,0:T(8,128)(2,1)} %param.17), channel_id=1, source_target_pairs={{2,0},{4,2},{6,4},{8,6},{10,8},{12,10},{14,12},{16,14},{18,16},{20... | collective-permute-start | bytes 3145736 | tf_op jit(solution)/shard_map/ppermute | solution.py:17
  129.6 19.4 %copy-start.3 = (bf16[8,2,64,512]{3,2,1,0:T(8,128)(2,1)S(1)}, bf16[8,2,64,512]{3,2,1,0:T(8,128)(2,1)}, u32[]{:S(2)}) copy-start(bf16[8,2,64,512]{3,2,1,0:T(8,128)(2,1)} %param.17) | copy-start | bytes 3145732
  164.6 1.3 copy-start.4
  200.2 39.2 %all-to-all-start = ((bf16[1,2,64,64,128]{4,2,1,0,3:T(8,128)(2,1)}), bf16[1,2,64,64,128]{4,2,1,0,3:T(8,128)(2,1)S(1)}, u32[]{:S(2)}, u32[]{:S(2)}) async-start(bf16[1,2,64,64,128]{4,2,1,0,3:T(8,128)(2,1)} %copy.61), calls=%async_computation | async-start | bytes 4194304 | tf_op jit(solution)/shard_map/all_to_all | solution.py:133
  241.8 4.6 %copy-start.1 = (bf16[316,2,512]{2,1,0:T(2,128)(2,1)S(1)}, bf16[316,2,512]{2,1,0:T(2,128)(2,1)}, u32[]{:S(2)}) copy-start(bf16[316,2,512]{2,1,0:T(2,128)(2,1)} %param.24) | copy-start | bytes 1941508
Sparse Core Ops, SparseCore 0:
  13.7 16.9 all-gather.1
  94.9 16.0 reduce-scatter.3
where the time goes:
time: 257 us; the launch traced here: 253 us
  local copies, waits for them, and re-layouts  79 us (31%)
  other arithmetic  62.1 us (24%)
  waiting for transfers between devices  49.3 us (19%)
  starting transfers between devices  24.2 us (9%)
  matrix products  24.2 us (9%)
  between operations  14.4 us (6%)
    unnamed x39, local copies, waits for them, and re-layouts  35.7 us
    convert_element_type x1, other arithmetic, local(): fetched = leaf_wide[il0_src - first_box].astype(jnp.float32)  18.8 us
    all_gather x1, waiting for transfers between devices, local(): full = lax.all_gather(leaf_out, 'dir', axis=3, tiled=True)  15.6 us
    ppermute x2, waiting for transfers between devices, padded(): lax.ppermute(tail, axis, [(i, (i + 1) % count) for i in range(ends)])  13.5 us
    reduce_sum x2, other arithmetic, translate(): jnp.sum(op_real * fetched[:, :, 0] - op_imag * fetched[:, :, 1], axis=1)  13.3 us
    all_to_all x1, starting transfers between devices, local(): lax.all_to_all(halved.astype(jnp.bfloat16), 'box', split_axis=3, concat_a...  12.1 us
    gather x1, local copies, waits for them, and re-layouts, local(): fetched = leaf_wide[il0_src - first_box].astype(jnp.float32)  10.3 us
    all_to_all x1, waiting for transfers between devices, local(): lax.all_to_all(halved.astype(jnp.bfloat16), 'box', split_axis=3, concat_a...  10.2 us
  transfers between devices with their start and end apart: 7, of which 6 were waited for; matrix products, arithmetic and copies ran while one was open for 28% of the time, Pallas kernels for 0%

commit v1 on v0

v1 whole, which is shorter than its diff:
```python
import jax
import jax.numpy as jnp
from jax import lax
from jax.experimental import pallas as pl
from jax.experimental.pallas import tpu as pltpu
from jax.sharding import Mesh
from jax.sharding import PartitionSpec as P

BOX = ("y", "xh", "xl", "z")
ALL = BOX + ("dir",)
F32 = jnp.float32
BF16 = jnp.bfloat16
VMEM_LIMIT = 48 * 1024 * 1024


def params():
    return pltpu.CompilerParams(vmem_limit_bytes=VMEM_LIMIT)


def cost(flops, nbytes):
    return pl.CostEstimate(flops=flops, bytes_accessed=nbytes, transcendentals=0)


def dot(a, b):
    return lax.dot_general(a, b, (((1,), (0,)), ((), ())), preferred_element_type=F32)


def dot_nt(a, b):
    return lax.dot_general(a, b, (((1,), (1,)), ((), ())), preferred_element_type=F32)


def leaf_kernel(dir_ref, src_ref, rad_ref, leaf_ref, send_ref):
    rows = src_ref[0].reshape(128, 512)
    first = dot(rows, rad_ref[0, 0])
    second = dot(rows, rad_ref[0, 1])
    leaf_ref[0, 0] = (first[:64] - second[64:]).astype(BF16)
    leaf_ref[0, 1] = (second[:64] + first[64:]).astype(BF16)
    start = pl.multiple_of((1 - dir_ref[0]) * 32, 32)
    send_ref[0] = leaf_ref[0, :, pl.ds(start, 32), :]


def leaf_patterns(dir_index, sources, radiation):
    return pl.pallas_call(
        leaf_kernel,
        grid_spec=pltpu.PrefetchScalarGridSpec(
            num_scalar_prefetch=1,
            grid=(8,),
            in_specs=[
                pl.BlockSpec((1, 2, 64, 512), lambda b, d: (b, 0, 0, 0)),
                pl.BlockSpec((1, 2, 512, 512), lambda b, d: (b, 0, 0, 0)),
            ],
            out_specs=[
                pl.BlockSpec((1, 2, 64, 512), lambda b, d: (b, 0, 0, 0)),
                pl.BlockSpec((1, 2, 32, 512), lambda b, d: (b, 0, 0, 0)),
            ],
        ),
        out_shape=[
            jax.ShapeDtypeStruct((8, 2, 64, 512), BF16),
            jax.ShapeDtypeStruct((8, 2, 32, 512), BF16),
        ],
        compiler_params=params(),
        cost_estimate=cost(2 * 8 * 4 * 64 * 512 * 512, 11 << 20),
        name="leaf_patterns",
    )(dir_index, sources, radiation)


def level_one_kernel(
    dir_ref, mine_ref, other_ref, phi_ref, theta_ref, shift_ref, out_ref, expand, near, far, phi4, rows_f32
):
    step = pl.program_id(0)
    dir_index = dir_ref[0]

    @pl.when(step == 0)
    def _():
        spread = (
            lax.broadcasted_iota(jnp.int32, (32, 2048), 0)
            == lax.broadcasted_iota(jnp.int32, (32, 2048), 1) // 64
        ).astype(F32).astype(BF16)
        expand[...] = lax.dot_general(
            theta_ref[...], spread, (((0,), (0,)), ((), ())), preferred_element_type=F32
        )
        phi4[...] = jnp.zeros_like(phi4)
        for s in range(4):
            phi4[64 * s : 64 * s + 64, 128 * s : 128 * s + 128] = phi_ref[...]

    diagonal = (
        lax.broadcasted_iota(jnp.int32, (64, 256), 0) == lax.broadcasted_iota(jnp.int32, (64, 256), 1) % 64
    )
    near_rows = pl.multiple_of(dir_index * 8, 8)
    far_rows = pl.multiple_of((1 - dir_index) * 8, 8)
    for part in range(4):
        lanes = pl.ds(pl.multiple_of(step * 1024 + part * 256, 256), 256)
        near_values = expand[pl.ds(near_rows, 8), lanes]
        far_values = expand[pl.ds(far_rows, 8), lanes]
        for t in range(8):
            near[64 * t : 64 * t + 64, :] = jnp.where(diagonal, near_values[t : t + 1], 0.0).astype(BF16)
            far[64 * t : 64 * t + 64, :] = jnp.where(diagonal, far_values[t : t + 1], 0.0).astype(BF16)
        theta_out = dot(mine_ref[...].reshape(512, 512), near[...]) + dot(
            other_ref[...].reshape(512, 512), far[...]
        )
        fine = dot(theta_out.astype(BF16), phi4[...])
        real_sum = jnp.zeros((32, 512), F32)
        imag_sum = jnp.zeros((32, 512), F32)
        for b in range(8):
            real_part = fine[64 * b : 64 * b + 32]
            imag_part = fine[64 * b + 32 : 64 * b + 64]
            factors = shift_ref[b, :, 512 * part : 512 * part + 512].astype(F32)
            f_real, f_imag = factors[0:1], factors[1:2]
            real_sum = real_sum + (real_part * f_real - imag_part * f_imag)
            imag_sum = imag_sum + (real_part * f_imag + imag_part * f_real)
        for s in range(4):
            rows_f32[0:32, 4 * part + s, :] = real_sum[:, 128 * s : 128 * s + 128]
            rows_f32[32:64, 4 * part + s, :] = imag_sum[:, 128 * s : 128 * s + 128]
    for d in range(8):
        out_ref[d, 0] = rows_f32[4 * d : 4 * d + 4].astype(BF16)
        out_ref[d, 1] = rows_f32[32 + 4 * d : 36 + 4 * d].astype(BF16)


def level_one_patterns(dir_index, leaf, received, phi, theta, shift):
    return pl.pallas_call(
        level_one_kernel,
        grid_spec=pltpu.PrefetchScalarGridSpec(
            num_scalar_prefetch=1,
            grid=(2,),
            in_specs=[
                pl.BlockSpec((8, 2, 32, 512), lambda i, d: (0, 0, d[0], 0)),
                pl.BlockSpec((8, 2, 32, 512), lambda i, d: (0, 0, 0, 0)),
                pl.BlockSpec((64, 128), lambda i, d: (0, 0)),
                pl.BlockSpec((32, 16), lambda i, d: (0, 0)),
                pl.BlockSpec((8, 2, 2048), lambda i, d: (0, 0, i)),
            ],
            out_specs=pl.BlockSpec((8, 2, 4, 16, 128), lambda i, d: (0, 0, 0, i, 0)),
            scratch_shapes=[
                pltpu.VMEM((16, 2048), F32),
                pltpu.VMEM((512, 256), BF16),
                pltpu.VMEM((512, 256), BF16),
                pltpu.VMEM((256, 512), BF16),
                pltpu.VMEM((64, 16, 128), F32),
            ],
        ),
        out_shape=jax.ShapeDtypeStruct((8, 2, 4, 32, 128), BF16),
        compiler_params=params(),
        cost_estimate=cost(4 << 30, 2 << 20),
        name="level_one",
    )(dir_index, leaf, received, phi, theta, shift)


def level_two_kernel(kids_ref, phi_ref, theta_ref, shift_ref, out_ref, blocks, total, turned):
    tiled = dot(
        theta_ref[...],
        (
            lax.broadcasted_iota(jnp.int32, (32, 256), 0)
            == lax.broadcasted_iota(jnp.int32, (32, 256), 1) % 32
        ).astype(F32).astype(BF16),
    )
    owner = lax.broadcasted_iota(jnp.int32, (64, 256), 1) // 32
    for m in range(8):
        blocks[64 * m : 64 * m + 64, :] = jnp.where(owner == m, tiled, 0.0).astype(BF16)
    total[...] = jnp.zeros_like(total)

    def child(o, carry):
        along_phi = dot(kids_ref[o].reshape(256, 128), phi_ref[...]).astype(BF16)
        along_theta = dot(blocks[...], along_phi)
        f_real = shift_ref[o, 0].astype(F32)
        f_imag = shift_ref[o, 1].astype(F32)
        for r in range(4):
            real_part = along_theta[64 * r : 64 * r + 64]
            imag_part = along_theta[256 + 64 * r : 320 + 64 * r]
            total[r] = total[r] + (real_part * f_real - imag_part * f_imag)
            total[4 + r] = total[4 + r] + (real_part * f_imag + imag_part * f_real)
        return carry

    lax.fori_loop(0, 8, child, 0)
    for m in range(8):
        turned[:, m, :] = total[m]
    out_ref[:, 0] = turned[:, :, 0:128].astype(BF16)
    out_ref[:, 1] = turned[:, :, 128:256].astype(BF16)


def level_two_terms(kids, phi, theta, shift):
    return pl.pallas_call(
        level_two_kernel,
        out_shape=jax.ShapeDtypeStruct((64, 2, 8, 128), BF16),
        in_specs=[pl.BlockSpec(memory_space=pltpu.VMEM)] * 4,
        out_specs=pl.BlockSpec(memory_space=pltpu.VMEM),
        scratch_shapes=[
            pltpu.VMEM((512, 256), BF16),
            pltpu.VMEM((8, 64, 256), F32),
            pltpu.VMEM((64, 8, 256), F32),
        ],
        compiler_params=params(),
        cost_estimate=cost(2 << 30, 2 << 20),
        name="level_two",
    )(kids, phi, theta, shift)


def upper_kernel(src_ref, rel_ref, got_ref, ops_ref, out_ref, plain, rolled):
    for h in range(8):
        for g in range(8):
            for d in range(2):
                tile = got_ref[h, g, d].astype(F32)
                plain[h, 2 * g + d] = tile
                rolled[h, 2 * g + d] = pltpu.roll(tile, 4, 0)
    low = lax.broadcasted_iota(jnp.int32, (8, 128), 0) < 4

    def one(h, carry):
        total = jnp.zeros((16, 8, 128), F32)
        for i in range(4):
            operator = ops_ref[rel_ref[h, i]].astype(F32)
            op_real = jnp.broadcast_to(operator[0:1], (8, 128))
            op_imag = jnp.broadcast_to(operator[1:2], (8, 128))
            op_imag = jnp.where(low, -op_imag, op_imag)
            src = src_ref[h, i]
            total = total + (plain[src] * op_real[None] + rolled[src] * op_imag[None])
        for g in range(8):
            for d in range(2):
                start = 32 * d + 4 * g
                out_ref[h, 0, start : start + 4, :] = total[2 * g + d, 0:4]
                out_ref[h, 1, start : start + 4, :] = total[2 * g + d, 4:8]
        return carry

    lax.fori_loop(0, 8, one, 0)


def upper_translate(il2_src, il2_rel, got, operators):
    smem = pl.BlockSpec(memory_space=pltpu.SMEM)
    vmem = pl.BlockSpec(memory_space=pltpu.VMEM)
    return pl.pallas_call(
        upper_kernel,
        out_shape=jax.ShapeDtypeStruct((8, 2, 64, 128), F32),
        in_specs=[smem, smem, vmem, vmem],
        out_specs=vmem,
        scratch_shapes=[pltpu.VMEM((8, 16, 8, 128), F32), pltpu.VMEM((8, 16, 8, 128), F32)],
        compiler_params=params(),
        cost_estimate=cost(1 << 26, 1 << 20),
        name="upper_translate",
    )(il2_src, il2_rel, got, operators)


def near_kernel(
    link_ref, dir_ref, blocks_ref, own_ref, left_ref, left2_ref, right_ref, right2_ref, out_ref, boxes, sems
):
    b = pl.program_id(0)

    @pl.when(b == 0)
    def _():
        mine = pl.multiple_of(dir_ref[0] * 4, 4)
        theirs = pl.multiple_of((1 - dir_ref[0]) * 4, 4)
        copies = [
            pltpu.make_async_copy(own_ref, boxes.at[pl.ds(8, 8)], sems.at[0]),
            pltpu.make_async_copy(left_ref, boxes.at[pl.ds(mine, 4)], sems.at[1]),
            pltpu.make_async_copy(left2_ref, boxes.at[pl.ds(theirs, 4)], sems.at[2]),
            pltpu.make_async_copy(right_ref, boxes.at[pl.ds(16 + mine, 4)], sems.at[3]),
            pltpu.make_async_copy(right2_ref, boxes.at[pl.ds(16 + theirs, 4)], sems.at[4]),
        ]
        for copy in copies:
            copy.start()
        for copy in copies:
            copy.wait()

    first = jnp.zeros((128, 256), F32)
    second = jnp.zeros((128, 256), F32)
    for j in range(3):
        rows = boxes[link_ref[b, j]].reshape(128, 512)
        first = first + dot_nt(rows, blocks_ref[0, j, 0])
        second = second + dot_nt(rows, blocks_ref[0, j, 1])
    out_ref[0, 0] = first[:64] - second[64:]
    out_ref[0, 1] = second[:64] + first[64:]


def near_products(links, dir_index, near_blocks, own, left, left2, right, right2):
    anywhere = pl.BlockSpec(memory_space=pl.ANY)
    return pl.pallas_call(
        near_kernel,
        grid_spec=pltpu.PrefetchScalarGridSpec(
            num_scalar_prefetch=2,
            grid=(8,),
            in_specs=[pl.BlockSpec((1, 3, 2, 256, 512), lambda b, l, d: (b, 0, 0, 0, 0))] + [anywhere] * 5,
            out_specs=pl.BlockSpec((1, 2, 64, 256), lambda b, l, d: (b, 0, 0, 0)),
            scratch_shapes=[pltpu.VMEM((24, 2, 64, 512), BF16), pltpu.SemaphoreType.DMA((5,))],
        ),
        out_shape=jax.ShapeDtypeStruct((8, 2, 64, 256), F32),
        compiler_params=params(),
        cost_estimate=cost(2 * 24 * 4 * 64 * 256 * 512, 17 << 20),
        name="near_field",
    )(links, dir_index, near_blocks, own, left, left2, right, right2)


def translate_kernel(link_ref, rel_ref, count_ref, ops_ref, own_ref, left_ref, right_ref, out_ref, boxes, wide, sems):
    b = pl.program_id(0)

    @pl.when(b == 0)
    def _():
        copies = [
            pltpu.make_async_copy(left_ref, boxes.at[pl.ds(0, 8)], sems.at[0]),
            pltpu.make_async_copy(own_ref, boxes.at[pl.ds(8, 8)], sems.at[1]),
            pltpu.make_async_copy(right_ref, boxes.at[pl.ds(16, 8)], sems.at[2]),
        ]
        for copy in copies:
            copy.start()
        for copy in copies:
            copy.wait()

    count = count_ref[b]

    def widen(i, carry):
        wide[i] = ops_ref[rel_ref[b, i]].astype(F32)
        return carry

    lax.fori_loop(0, count, widen, 0)
    for chunk in range(4):
        rows = slice(16 * chunk, 16 * chunk + 16)

        def one(i, carry):
            real_sum, imag_sum = carry
            link = link_ref[b, i]
            real_part = boxes[link, 0, rows, :].astype(F32)
            imag_part = boxes[link, 1, rows, :].astype(F32)
            op_real = wide[i, 0:1, :]
            op_imag = wide[i, 1:2, :]
            real_sum = real_sum + (op_real * real_part - op_imag * imag_part)
            imag_sum = imag_sum + (op_real * imag_part + op_imag * real_part)
            return real_sum, imag_sum

        zero = jnp.zeros((16, 512), F32)
        real_sum, imag_sum = lax.fori_loop(0, count, one, (zero, zero))
        out_ref[0, 0, rows, :] = real_sum
        out_ref[0, 1, rows, :] = imag_sum


def leaf_translate(links, rel, count, operators, own, left, right):
    anywhere = pl.BlockSpec(memory_space=pl.ANY)
    return pl.pallas_call(
        translate_kernel,
        grid_spec=pltpu.PrefetchScalarGridSpec(
            num_scalar_prefetch=3,
            grid=(8,),
            in_specs=[pl.BlockSpec((316, 2, 512), lambda b, l, r, c: (0, 0, 0))] + [anywhere] * 3,
            out_specs=pl.BlockSpec((1, 2, 64, 512), lambda b, l, r, c: (b, 0, 0, 0)),
            scratch_shapes=[
                pltpu.VMEM((24, 2, 64, 512), BF16),
                pltpu.VMEM((16, 2, 512), F32),
                pltpu.SemaphoreType.DMA((3,)),
            ],
        ),
        out_shape=jax.ShapeDtypeStruct((8, 2, 64, 512), F32),
        compiler_params=params(),
        cost_estimate=cost(1 << 30, 6 << 20),
        name="leaf_translate",
    )(links, rel, count, operators, own, left, right)


def local(
    sources,
    near_blocks,
    near_src,
    radiation,
    il0_src,
    il0_rel,
    il0_count,
    trans0,
    phi_interp1,
    theta_interp1,
    shift1,
    phi_interp2,
    theta_interp2,
    shift2,
    il2_src,
    il2_rel,
    trans2,
):
    box_index = lax.axis_index(BOX)
    dir_position = lax.axis_index("dir")
    dir_index = dir_position.astype(jnp.int32).reshape(1)
    owners = lax.axis_size(BOX)
    first_box = (box_index - 1) * 8
    to_right = [(i, (i + 1) % owners) for i in range(owners)]
    to_left = [((i + 1) % owners, i) for i in range(owners)]
    swap = [(0, 1), (1, 0)]

    half = lax.dynamic_slice_in_dim(sources, dir_position * 4, 4, 0)
    left = lax.ppermute(half, BOX, to_right)
    right = lax.ppermute(half, BOX, to_left)
    left2 = lax.ppermute(left, "dir", swap)
    right2 = lax.ppermute(right, "dir", swap)

    leaf, send = leaf_patterns(dir_index, sources, radiation)
    leaf_left = lax.ppermute(leaf, BOX, to_right)
    leaf_right = lax.ppermute(leaf, BOX, to_left)
    received = lax.ppermute(send, "dir", swap)

    level_one = level_one_patterns(dir_index, leaf, received, phi_interp1, theta_interp1, shift1)
    kids = lax.all_to_all(level_one, ("xl", "z"), 0, 0, tiled=True)
    terms = level_two_terms(kids, phi_interp2, theta_interp2, shift2.reshape(8, 2, 64, 256))
    got = lax.all_to_all(terms.reshape(128, 8, 128), ALL, 0, 0, tiled=True)

    near_field = near_products(
        (near_src - first_box).astype(jnp.int32), dir_index, near_blocks, sources, left, left2, right, right2
    )
    leaf_incoming = leaf_translate(
        (il0_src - first_box).astype(jnp.int32), il0_rel, il0_count, trans0, leaf, leaf_left, leaf_right
    )
    upper = upper_translate(il2_src, il2_rel, got.reshape(8, 8, 2, 8, 128), trans2.reshape(316, 2, 128))
    return near_field, leaf_incoming, upper.reshape(8, 2, 64, 1, 128)


def solution(mesh):
    fine = Mesh(mesh.devices.reshape(4, 2, 2, 4, 2), ALL)
    placed = (
        P(BOX, None, None, None),
        P(BOX, None, None, "dir", None),
        P(BOX, None),
        P(BOX, None, None, "dir"),
        P(BOX, None),
        P(BOX, None),
        P(BOX),
        P(None, None, "dir"),
        P(),
        P(),
        P(),
        P(),
        P(),
        P(),
        P(),
        P(),
        P(None, None, BOX, "dir"),
    )
    return jax.shard_map(
        local,
        mesh=fine,
        in_specs=placed,
        out_specs=(
            P(BOX, None, None, "dir"),
            P(BOX, None, None, "dir"),
            P(None, None, None, BOX, "dir"),
        ),
        check_vma=False,
    )
```

time: 257 us -> 107 us (0.42)
  local copies, waits for them, and re-layouts: 79 us -> 9.21 us
  other arithmetic: 62.1 us -> 0.01 us
  Pallas kernels: 0 us -> 45.9 us
  waiting for transfers between devices: 49.3 us -> 23.9 us
  matrix products: 24.2 us -> 0 us
  between operations: 14.4 us -> 0.87 us
    pallas_call x0 -> x6, Pallas kernels: none -> 45.9 us  [the longest x1 12.4 us: near_products(): pl.pallas_call(near_kernel, grid_spec=pltpu.PrefetchScalarGridSpec(num_sc...]
    unnamed x39 -> x41, local copies, waits for them, and re-layouts: 35.7 us -> 6.21 us
    dot_general x4 -> x0, matrix products: 24.2 us -> none  [the longest x1 8.08 us: local(): jnp.einsum('bjcqp,bjerp->bcerq', near_blocks, picked, preferred_element_t...]
    ppermute x4 -> x7, waiting for transfers between devices: 23.6 us -> 0.02 us  [the longest x1 0.01 us: local(): right = lax.ppermute(half, BOX, to_left)]
    convert_element_type x6 -> x0, other arithmetic: 22.3 us -> none  [the longest x1 18.8 us: local(): fetched = leaf_wide[il0_src - first_box].astype(jnp.float32)]
    reduce_sum x4 -> x0, other arithmetic: 20.9 us -> none  [the longest x2 13.3 us: translate(): jnp.sum(op_real * fetched[:, :, 0] - op_imag * fetched[:, :, 1], axis=1)]
    gather x5 -> x0, local copies, waits for them, and re-layouts: 18.1 us -> none  [the longest x1 10.3 us: local(): fetched = leaf_wide[il0_src - first_box].astype(jnp.float32)]
    all_gather x1 -> x0, waiting for transfers between devices: 15.6 us -> none  [local(): full = lax.all_gather(leaf_out, 'dir', axis=3, tiled=True)]
  transfers between devices with their start and end apart: 7 -> 9, of which waited for: 6 -> 1; matrix products, arithmetic and copies ran while one was open for 28% -> 3% of each run, Pallas kernels for 0% -> 34%
where the time goes in v1:
time: 107 us; the launch traced here: 106 us
  Pallas kernels  45.9 us (43%)
  starting transfers between devices  25.9 us (24%)
  waiting for transfers between devices  23.9 us (22%)
  local copies, waits for them, and re-layouts  9.21 us (9%)
    all_to_all x1, waiting for transfers between devices, local(): kids = lax.all_to_all(level_one, ('xl', 'z'), 0, 0, tiled=True)  23.9 us
    pallas_call x1, Pallas kernels, near_products(): pl.pallas_call(near_kernel, grid_spec=pltpu.PrefetchScalarGridSpec(num_sc...  12.4 us
    pallas_call x1, Pallas kernels, leaf_translate(): pl.pallas_call(translate_kernel, grid_spec=pltpu.PrefetchScalarGridSpec(n...  10.6 us
    ppermute x1, starting transfers between devices, local(): right = lax.ppermute(half, BOX, to_left)  8.49 us
    pallas_call x1, Pallas kernels, level_one_patterns(): pl.pallas_call(level_one_kernel, grid_spec=pltpu.PrefetchScalarGridSpec(n...  8.28 us
    pallas_call x1, Pallas kernels, leaf_patterns(): pl.pallas_call(leaf_kernel, grid_spec=pltpu.PrefetchScalarGridSpec(num_sc...  7.81 us
    ppermute x1, starting transfers between devices, local(): leaf_right = lax.ppermute(leaf, BOX, to_left)  6.89 us
    unnamed x41, local copies, waits for them, and re-layouts  6.21 us
  transfers between devices with their start and end apart: 9, of which 1 were waited for; matrix products, arithmetic and copies ran while one was open for 3% of the time, Pallas kernels for 34%

profile of v1, /device:TPU:1, one launch (start us, length us, event | category | flops | bytes accessed | tf_op | source)
XLA Modules:
  0.0 105.8 jit_solution(3690602858443579076)
XLA Ops:
  0.6 0.0 copy-start.13
  0.6 0.0 copy-start
  0.7 1.2 %copy-done = bf16[8,2,64,512]{3,2,1,0:T(8,128)(2,1)S(1)} copy-done((bf16[8,2,64,512]{3,2,1,0:T(8,128)(2,1)S(1)}, bf16[8,2,64,512]{3,2,1,0:T(8,128)(2,1)}, u32[]{:S(2)}) %copy-start) | copy-done | bytes 1048600
  1.9 0.0 copy-start.1
  1.9 0.0 copy-start.9
  1.9 0.0 copy-start.11
  1.9 7.8 %leaf_patterns.1 = (bf16[8,2,64,512]{3,2,1,0:T(8,128)(2,1)S(1)}, bf16[8,2,32,512]{3,2,1,0:T(8,128)(2,1)}) custom-call(s32[1]{0:T(128)} %bitcast.dir_ref, bf16[8,2,64,512]{3,2,1,0:T(8,128)(2,1)S(1)} %copy-done, bf16[8,2,512,512]{3,2,1,0:T(8,128)(2,1)} %rad_ref.1), custom_call_target="tpu_custom_call" | custom-call | flops 1073741824 | bytes 11534336 | tf_op jit(solution)/shard_map/leaf_patterns/pallas_call | solution.py:43
  9.7 1.4 %collective-permute-start.6 = (bf16[8,2,32,512]{3,2,1,0:T(8,128)(2,1)}, bf16[8,2,32,512]{3,2,1,0:T(8,128)(2,1)}, u32[]{:S(2)}, u32[]{:S(2)}) collective-permute-start(bf16[8,2,32,512]{3,2,1,0:T(8,128)(2,1)} %get-tuple-element.6), channel_id=1, source_target_pairs={{0,1},{1,0},{2,3},{3,2},{4,5},{5,4},{6,7},{7,6},{8,9},{9,8},{10,11... | collective-permute-start | bytes 1572872 | tf_op jit(solution)/shard_map/ppermute | solution.py:390
  11.1 0.0 copy-done.1
  11.1 0.8 constant_dynamic-slice_fusion
  11.9 8.5 %collective-permute-start.2 = (bf16[4,2,64,512]{3,2,1,0:T(8,128)(2,1)}, bf16[4,2,64,512]{3,2,1,0:T(8,128)(2,1)}, u32[]{:S(2)}, u32[]{:S(2)}) collective-permute-start(bf16[4,2,64,512]{3,2,1,0:T(8,128)(2,1)} %constant_dynamic-slice_fusion), channel_id=1, source_target_pairs={{2,0},{4,2},{6,4},{8,6},{10,8},{12,10},{14,12},{16,14},{18,16},{20... | collective-permute-start | bytes 1572872 | tf_op jit(solution)/shard_map/ppermute | solution.py:383
  20.4 0.0 collective-permute-start
  20.4 6.9 %collective-permute-start.5 = (bf16[8,2,64,512]{3,2,1,0:T(8,128)(2,1)S(1)}, bf16[8,2,64,512]{3,2,1,0:T(8,128)(2,1)S(1)}, u32[]{:S(2)}, u32[]{:S(2)}) collective-permute-start(bf16[8,2,64,512]{3,2,1,0:T(8,128)(2,1)S(1)} %get-tuple-element.5.own_ref.mine_ref), channel_id=1, source_target_pairs={{2,0},{4,2},{6,4},{8,6},{10,8},{12,10},{14,12},{16,14},{18,16},{20... | collective-permute-start | bytes 3145736 | tf_op jit(solution)/shard_map/ppermute | solution.py:389
  27.3 0.0 collective-permute-start.4
  27.3 0.0 copy-done.13
  27.3 0.1 copy.21.theta_ref
  27.4 0.0 copy-start.15
  27.4 0.0 copy-start.12
  27.4 0.0 copy-start.10
  27.4 0.0 collective-permute-done.6.other_ref
  27.4 0.0 copy-done.9
  27.5 0.0 copy-done.11
  27.5 8.3 %level_one.1 = bf16[8,2,4,32,128]{4,3,2,1,0:T(8,128)(2,1)S(1)} custom-call(s32[1]{0:T(128)} %bitcast.dir_ref, bf16[8,2,64,512]{3,2,1,0:T(8,128)(2,1)S(1)} %get-tuple-element.5.own_ref.mine_ref, bf16[8,2,32,512]{3,2,1,0:T(8,128)(2,1)} %collective-permute-done.6.other_ref, bf16[64,128]{1,0:T(8,128)(2,1)S(1)} %copy-done.11, bf16[32,16]{1,0:T(8,128)(2,1)S(1)} %copy.21.theta_ref, ...), custom_call_target="tpu_custom_call" | custom-call | flops 4294967296 | bytes 2097152 | tf_op jit(solution)/shard_map/level_one/pallas_call | solution.py:120
  35.8 0.0 copy-start.3
  35.8 0.8 copy-done.3
  36.6 0.0 copy-start.14
  36.6 0.0 copy-start.16
  36.6 0.0 copy-start.8
  36.6 4.3 %all-to-all-start = ((bf16[8,2,4,32,128]{4,3,2,1,0:T(8,128)(2,1)}), bf16[8,2,4,32,128]{4,3,2,1,0:T(8,128)(2,1)}, u32[]{:S(2)}, u32[]{:S(2)}) async-start(bf16[8,2,4,32,128]{4,3,2,1,0:T(8,128)(2,1)} %copy-done.3), calls=%async_computation | async-start | bytes 1048576 | tf_op jit(solution)/shard_map/all_to_all | solution.py:393
  40.9 0.0 copy-done.15
  40.9 0.1 copy.20
  41.0 0.0 copy-done.12
  41.0 0.1 copy.22.theta_ref
  41.1 2.2 %reshape.25.shift_ref = bf16[8,2,64,256]{3,2,1,0:T(8,128)(2,1)} reshape(bf16[8,2,16384]{2,1,0:T(2,128)(2,1)} %param.30) | data formatting | bytes 1048576 | tf_op jit(solution)/shard_map/reshape | solution.py:394
  43.2 0.0 collective-permute-done.2.right_ref
  43.3 0.8 collective-permute-start.3
  44.1 0.0 collective-permute-done.left_ref
  44.1 0.1 collective-permute-start.1
  44.2 23.9 %all-to-all-done.kids_ref = bf16[8,2,4,32,128]{4,3,2,1,0:T(8,128)(2,1)} async-done(((bf16[8,2,4,32,128]{4,3,2,1,0:T(8,128)(2,1)}), bf16[8,2,4,32,128]{4,3,2,1,0:T(8,128)(2,1)}, u32[]{:S(2)}, u32[]{:S(2)}) %all-to-all-start) | async-done | bytes 524320 | tf_op jit(solution)/shard_map/all_to_all | solution.py:393
  68.1 0.0 copy-done.10
  68.1 1.0 copy-done.4
  69.2 4.9 %level_two.1 = bf16[64,2,8,128]{3,2,1,0:T(8,128)(2,1)S(1)} custom-call(bf16[8,2,4,32,128]{4,3,2,1,0:T(8,128)(2,1)} %all-to-all-done.kids_ref, bf16[128,256]{1,0:T(8,128)(2,1)S(1)} %copy-done.10, bf16[64,32]{1,0:T(8,128)(2,1)S(1)} %copy.22.theta_ref, bf16[8,2,64,256]{3,2,1,0:T(8,128)(2,1)S(1)} %copy-done.4), custom_call_target="tpu_custom_call" | custom-call | flops 2147483648 | bytes 2097152 | tf_op jit(solution)/shard_map/level_two/pallas_call | solution.py:181
  74.0 0.0 copy-start.5
  74.0 0.7 copy-done.5
  74.7 3.9 %all-to-all-start.1 = ((bf16[128,8,128]{2,1,0:T(8,128)(2,1)}), bf16[128,8,128]{2,1,0:T(8,128)(2,1)S(1)}, u32[]{:S(2)}, u32[]{:S(2)}) async-start(bf16[128,8,128]{2,1,0:T(8,128)(2,1)} %bitcast.8), calls=%async_computation.1 | async-start | bytes 524288 | tf_op jit(solution)/shard_map/all_to_all | solution.py:395
  78.6 0.0 copy-done.14
  78.7 0.0 copy-done.16
  78.7 0.1 copy.23.src_ref
  78.8 0.0 copy-done.17
  78.8 0.1 copy.24.rel_ref
  78.8 0.0 collective-permute-done.5.right_ref
  78.8 0.0 collective-permute-done.4.left_ref
  78.8 0.0 copy-done.7
  78.9 0.0 copy-done.8
  78.9 0.0 copy-start.2
  78.9 1.1 %copy-done.2 = bf16[316,2,512]{2,1,0:T(2,128)(2,1)S(1)} copy-done((bf16[316,2,512]{2,1,0:T(2,128)(2,1)S(1)}, bf16[316,2,512]{2,1,0:T(2,128)(2,1)}, u32[]{:S(2)}) %copy-start.2) | copy-done | bytes 647192
  80.0 10.6 %leaf_translate.1 = f32[8,2,64,512]{3,2,1,0:T(8,128)} custom-call(s32[8,16]{1,0:T(8,128)S(1)} %broadcast_subtract_fusion.link_ref, s32[8,16]{1,0:T(8,128)S(1)} %copy-done.7, s32[8]{0:T(128)S(1)} %copy-done.8, bf16[316,2,512]{2,1,0:T(2,128)(2,1)S(1)} %copy-done.2, bf16[8,2,64,512]{3,2,1,0:T(8,128)(2,1)S(1)} %get-tuple-element.5.own_ref.mine_ref, ...), custom_call_target="tpu_custom_call" | custom-call | flops 1073741824 | bytes 6291456 | tf_op jit(solution)/shard_map/leaf_translate/pallas_call | solution.py:333
  90.5 0.0 collective-permute-done.3.right2_ref
  90.5 0.0 collective-permute-done.1.left2_ref
  90.6 12.4 %near_field.1 = f32[8,2,64,256]{3,2,1,0:T(8,128)} custom-call(s32[8,3]{1,0:T(8,128)S(1)} %broadcast_subtract_fusion.1.link_ref, s32[1]{0:T(128)} %bitcast.dir_ref, bf16[8,3,2,256,512]{4,3,2,1,0:T(8,128)(2,1)} %blocks_ref.1, bf16[8,2,64,512]{3,2,1,0:T(8,128)(2,1)S(1)} %copy-done.1, bf16[4,2,64,512]{3,2,1,0:T(8,128)(2,1)} %collective-permute-done.left_ref, ...), custom_call_target="tpu_custom_call" | custom-call | flops 1610612736 | bytes 17825792 | tf_op jit(solution)/shard_map/near_field/pallas_call | solution.py:273
  103.0 0.0 all-to-all-done.1
  103.0 0.0 copy-start.6
  103.0 0.9 copy-done.6
  103.9 1.9 %upper_translate.1 = f32[8,2,64,128]{3,2,1,0:T(8,128)} custom-call(s32[8,4]{1,0:T(8,128)S(1)} %copy.23.src_ref, s32[8,4]{1,0:T(8,128)S(1)} %copy.24.rel_ref, bf16[8,8,2,8,128]{4,3,2,1,0:T(8,128)(2,1)S(1)} %bitcast.7, bf16[316,2,128]{2,1,0:T(2,128)(2,1)S(1)} %bitcast.9), custom_call_target="tpu_custom_call" | custom-call | flops 67108864 | bytes 1048576 | tf_op jit(solution)/shard_map/upper_translate/pallas_call | solution.py:228
  (5 shorter events, 0.0 us)
Async XLA Ops:
  0.6 26.7 %copy-start.13 = (bf16[32,16]{0,1:T(8,128)(2,1)S(1)}, bf16[32,16]{0,1:T(8,128)(2,1)}, u32[]{:S(2)}) copy-start(bf16[32,16]{0,1:T(8,128)(2,1)} %param.26) | copy-start | bytes 3076
  0.6 1.2 %copy-start = (bf16[8,2,64,512]{3,2,1,0:T(8,128)(2,1)S(1)}, bf16[8,2,64,512]{3,2,1,0:T(8,128)(2,1)}, u32[]{:S(2)}) copy-start(bf16[8,2,64,512]{3,2,1,0:T(8,128)(2,1)} %src_ref.2) | copy-start | bytes 3145732
  1.9 9.2 %copy-start.1 = (bf16[8,2,64,512]{3,2,1,0:T(8,128)(2,1)S(1)}, bf16[8,2,64,512]{3,2,1,0:T(8,128)(2,1)}, u32[]{:S(2)}) copy-start(bf16[8,2,64,512]{3,2,1,0:T(8,128)(2,1)} %src_ref.2) | copy-start | bytes 3145732
  1.9 25.6 %copy-start.9 = (bf16[8,2,4096]{2,1,0:T(2,128)(2,1)S(1)}, bf16[8,2,4096]{2,1,0:T(2,128)(2,1)}, u32[]{:S(2)}) copy-start(bf16[8,2,4096]{2,1,0:T(2,128)(2,1)} %shift_ref.1) | copy-start | bytes 393220
  1.9 25.6 %copy-start.11 = (bf16[64,128]{1,0:T(8,128)(2,1)S(1)}, bf16[64,128]{1,0:T(8,128)(2,1)}, u32[]{:S(2)}) copy-start(bf16[64,128]{1,0:T(8,128)(2,1)} %phi_ref.2) | copy-start | bytes 49156
  9.7 17.7 %collective-permute-start.6 = (bf16[8,2,32,512]{3,2,1,0:T(8,128)(2,1)}, bf16[8,2,32,512]{3,2,1,0:T(8,128)(2,1)}, u32[]{:S(2)}, u32[]{:S(2)}) collective-permute-start(bf16[8,2,32,512]{3,2,1,0:T(8,128)(2,1)} %get-tuple-element.6), channel_id=1, source_target_pairs={{0,1},{1,0},{2,3},{3,2},{4,5},{5,4},{6,7},{7,6},{8,9},{9,8},{10,11... | collective-permute-start | bytes 1572872 | tf_op jit(solution)/shard_map/ppermute | solution.py:390
  11.9 31.3 %collective-permute-start.2 = (bf16[4,2,64,512]{3,2,1,0:T(8,128)(2,1)}, bf16[4,2,64,512]{3,2,1,0:T(8,128)(2,1)}, u32[]{:S(2)}, u32[]{:S(2)}) collective-permute-start(bf16[4,2,64,512]{3,2,1,0:T(8,128)(2,1)} %constant_dynamic-slice_fusion), channel_id=1, source_target_pairs={{2,0},{4,2},{6,4},{8,6},{10,8},{12,10},{14,12},{16,14},{18,16},{20... | collective-permute-start | bytes 1572872 | tf_op jit(solution)/shard_map/ppermute | solution.py:383
  20.4 23.7 %collective-permute-start = (bf16[4,2,64,512]{3,2,1,0:T(8,128)(2,1)}, bf16[4,2,64,512]{3,2,1,0:T(8,128)(2,1)}, u32[]{:S(2)}, u32[]{:S(2)}) collective-permute-start(bf16[4,2,64,512]{3,2,1,0:T(8,128)(2,1)} %constant_dynamic-slice_fusion), channel_id=1, source_target_pairs={{0,2},{2,4},{4,6},{6,8},{8,10},{10,12},{12,14},{14,16},{16,18},{18... | collective-permute-start | bytes 1572872 | tf_op jit(solution)/shard_map/ppermute | solution.py:382
  20.4 58.4 %collective-permute-start.5 = (bf16[8,2,64,512]{3,2,1,0:T(8,128)(2,1)S(1)}, bf16[8,2,64,512]{3,2,1,0:T(8,128)(2,1)S(1)}, u32[]{:S(2)}, u32[]{:S(2)}) collective-permute-start(bf16[8,2,64,512]{3,2,1,0:T(8,128)(2,1)S(1)} %get-tuple-element.5.own_ref.mine_ref), channel_id=1, source_target_pairs={{2,0},{4,2},{6,4},{8,6},{10,8},{12,10},{14,12},{16,14},{18,16},{20... | collective-permute-start | bytes 3145736 | tf_op jit(solution)/shard_map/ppermute | solution.py:389
  27.3 51.5 %collective-permute-start.4 = (bf16[8,2,64,512]{3,2,1,0:T(8,128)(2,1)S(1)}, bf16[8,2,64,512]{3,2,1,0:T(8,128)(2,1)}, u32[]{:S(2)}, u32[]{:S(2)}) collective-permute-start(bf16[8,2,64,512]{3,2,1,0:T(8,128)(2,1)S(1)} %get-tuple-element.5.own_ref.mine_ref), channel_id=1, source_target_pairs={{0,2},{2,4},{4,6},{6,8},{8,10},{10,12},{12,14},{14,16},{16,18},{18... | collective-permute-start | bytes 3145736 | tf_op jit(solution)/shard_map/ppermute | solution.py:388
  27.4 13.5 %copy-start.15 = (s32[8,3]{0,1:T(4,128)S(1)}, s32[8,3]{0,1:T(4,128)}, u32[]{:S(2)}) copy-start(s32[8,3]{0,1:T(4,128)} %param.19) | copy-start | bytes 292
  27.4 13.5 %copy-start.12 = (bf16[64,32]{0,1:T(8,128)(2,1)S(1)}, bf16[64,32]{0,1:T(8,128)(2,1)}, u32[]{:S(2)}) copy-start(bf16[64,32]{0,1:T(8,128)(2,1)} %param.29) | copy-start | bytes 12292
  27.4 40.7 %copy-start.10 = (bf16[128,256]{1,0:T(8,128)(2,1)S(1)}, bf16[128,256]{1,0:T(8,128)(2,1)}, u32[]{:S(2)}) copy-start(bf16[128,256]{1,0:T(8,128)(2,1)} %phi_ref.3) | copy-start | bytes 196612
  35.8 0.8 copy-start.3
  36.6 42.1 %copy-start.14 = (s32[8,16]{1,0:T(8,128)S(1)}, s32[8,16]{1,0:T(8,128)}, u32[]{:S(2)}) copy-start(s32[8,16]{1,0:T(8,128)} %param.21) | copy-start | bytes 1540
  36.6 42.1 %copy-start.16 = (s32[8,4]{0,1:T(4,128)S(1)}, s32[8,4]{0,1:T(4,128)}, u32[]{:S(2)}) copy-start(s32[8,4]{0,1:T(4,128)} %param.31) | copy-start | bytes 388
  36.6 42.2 %copy-start.17 = (s32[8,4]{0,1:T(4,128)S(1)}, s32[8,4]{0,1:T(4,128)}, u32[]{:S(2)}) copy-start(s32[8,4]{0,1:T(4,128)} %param.32) | copy-start | bytes 388
  36.6 42.3 %copy-start.7 = (s32[8,16]{1,0:T(8,128)S(1)}, s32[8,16]{1,0:T(8,128)}, u32[]{:S(2)}) copy-start(s32[8,16]{1,0:T(8,128)} %rel_ref.2) | copy-start | bytes 1540
  36.6 42.3 %copy-start.8 = (s32[8]{0:T(128)S(1)}, s32[8]{0:T(128)}, u32[]{:S(2)}) copy-start(s32[8]{0:T(128)} %count_ref.1) | copy-start | bytes 100
  36.6 31.5 %all-to-all-start = ((bf16[8,2,4,32,128]{4,3,2,1,0:T(8,128)(2,1)}), bf16[8,2,4,32,128]{4,3,2,1,0:T(8,128)(2,1)}, u32[]{:S(2)}, u32[]{:S(2)}) async-start(bf16[8,2,4,32,128]{4,3,2,1,0:T(8,128)(2,1)} %copy-done.3), calls=%async_computation | async-start | bytes 1048576 | tf_op jit(solution)/shard_map/all_to_all | solution.py:393
  43.3 47.3 %collective-permute-start.3 = (bf16[4,2,64,512]{3,2,1,0:T(8,128)(2,1)}, bf16[4,2,64,512]{3,2,1,0:T(8,128)(2,1)}, u32[]{:S(2)}, u32[]{:S(2)}) collective-permute-start(bf16[4,2,64,512]{3,2,1,0:T(8,128)(2,1)} %collective-permute-done.2.right_ref), channel_id=1, source_target_pairs={{0,1},{1,0},{2,3},{3,2},{4,5},{5,4},{6,7},{7,6},{8,9},{9,8},{10,11... | collective-permute-start | bytes 1572872 | tf_op jit(solution)/shard_map/ppermute | solution.py:385
  44.1 46.4 %collective-permute-start.1 = (bf16[4,2,64,512]{3,2,1,0:T(8,128)(2,1)}, bf16[4,2,64,512]{3,2,1,0:T(8,128)(2,1)}, u32[]{:S(2)}, u32[]{:S(2)}) collective-permute-start(bf16[4,2,64,512]{3,2,1,0:T(8,128)(2,1)} %collective-permute-done.left_ref), channel_id=1, source_target_pairs={{0,1},{1,0},{2,3},{3,2},{4,5},{5,4},{6,7},{7,6},{8,9},{9,8},{10,11... | collective-permute-start | bytes 1572872 | tf_op jit(solution)/shard_map/ppermute | solution.py:384
  68.1 1.0 copy-start.4
  74.0 0.7 copy-start.5
  74.7 28.2 %all-to-all-start.1 = ((bf16[128,8,128]{2,1,0:T(8,128)(2,1)}), bf16[128,8,128]{2,1,0:T(8,128)(2,1)S(1)}, u32[]{:S(2)}, u32[]{:S(2)}) async-start(bf16[128,8,128]{2,1,0:T(8,128)(2,1)} %bitcast.8), calls=%async_computation.1 | async-start | bytes 524288 | tf_op jit(solution)/shard_map/all_to_all | solution.py:395
  78.9 1.1 %copy-start.2 = (bf16[316,2,512]{2,1,0:T(2,128)(2,1)S(1)}, bf16[316,2,512]{2,1,0:T(2,128)(2,1)}, u32[]{:S(2)}) copy-start(bf16[316,2,512]{2,1,0:T(2,128)(2,1)} %ops_ref.1) | copy-start | bytes 1941508
  103.0 0.9 copy-start.6

commit v2 on v1

v2 whole, which is shorter than its diff:
```python
import functools

import jax
import jax.numpy as jnp
from jax import lax
from jax.experimental import pallas as pl
from jax.experimental.pallas import tpu as pltpu
from jax.sharding import Mesh
from jax.sharding import PartitionSpec as P

BOX = ("y", "xh", "xl", "z")
ALL = BOX + ("dir",)
F32 = jnp.float32
BF16 = jnp.bfloat16
HBM = pl.BlockSpec(memory_space=pltpu.HBM)
VMEM = pl.BlockSpec(memory_space=pltpu.VMEM)
SMEM = pl.BlockSpec(memory_space=pltpu.SMEM)
ANYWHERE = pl.BlockSpec(memory_space=pl.ANY)


def params(mebibytes):
    return pltpu.CompilerParams(vmem_limit_bytes=mebibytes << 20)


def cost(flops, nbytes):
    return pl.CostEstimate(flops=flops, bytes_accessed=nbytes, transcendentals=0)


def in_hbm(x):
    return pltpu.with_memory_space_constraint(x, pltpu.HBM)


def dot(a, b):
    return lax.dot_general(a, b, (((1,), (0,)), ((), ())), preferred_element_type=F32)


def dot_nt(a, b):
    return lax.dot_general(a, b, (((1,), (1,)), ((), ())), preferred_element_type=F32)


def leaf_kernel(
    dir_ref,
    src_hbm,
    rad_hbm,
    half_hbm,
    send_hbm,
    low_ref,
    high_ref,
    mine_ref,
    src,
    rad,
    leaf,
    src_sem,
    half_sem,
    rad_sems,
    send_sems,
):
    src_copy = pltpu.make_async_copy(src_hbm, src, src_sem)
    src_copy.start()
    for b in range(8):
        pltpu.make_async_copy(rad_hbm.at[b], rad.at[b], rad_sems.at[b]).start()
    src_copy.wait()
    first_box = pl.multiple_of(dir_ref[0] * 4, 4)
    half_copy = pltpu.make_async_copy(src.at[pl.ds(first_box, 4)], half_hbm, half_sem)
    half_copy.start()
    mine = pl.multiple_of(dir_ref[0] * 32, 32)
    other = pl.multiple_of((1 - dir_ref[0]) * 32, 32)

    def send(b):
        return pltpu.make_async_copy(leaf.at[b, :, pl.ds(other, 32), :], send_hbm.at[b], send_sems.at[b])

    def box(b, carry):
        pltpu.make_async_copy(rad_hbm.at[b], rad.at[b], rad_sems.at[b]).wait()
        rows = src[b].reshape(128, 512)
        first = dot(rows, rad[b, 0])
        second = dot(rows, rad[b, 1])
        leaf[b, 0] = (first[:64] - second[64:]).astype(BF16)
        leaf[b, 1] = (second[:64] + first[64:]).astype(BF16)
        send(b).start()
        low_ref[b] = leaf[b, :, :32, :]
        high_ref[b] = leaf[b, :, 32:, :]
        mine_ref[b] = leaf[b, :, pl.ds(mine, 32), :]
        return carry

    lax.fori_loop(0, 8, box, 0)
    half_copy.wait()
    for b in range(8):
        send(b).wait()


def leaf_patterns(dir_index, sources, radiation):
    return pl.pallas_call(
        leaf_kernel,
        in_specs=[SMEM, HBM, HBM],
        out_specs=[HBM, HBM, VMEM, VMEM, VMEM],
        out_shape=[jax.ShapeDtypeStruct((4, 2, 64, 512), BF16)]
        + [jax.ShapeDtypeStruct((8, 2, 32, 512), BF16)] * 4,
        scratch_shapes=[
            pltpu.VMEM((8, 2, 64, 512), BF16),
            pltpu.VMEM((8, 2, 512, 512), BF16),
            pltpu.VMEM((8, 2, 64, 512), BF16),
            pltpu.SemaphoreType.DMA,
            pltpu.SemaphoreType.DMA,
            pltpu.SemaphoreType.DMA((8,)),
            pltpu.SemaphoreType.DMA((8,)),
        ],
        compiler_params=params(16),
        cost_estimate=cost(1, 1),
        name="leaf_patterns",
    )(dir_index, in_hbm(sources), in_hbm(radiation))


def level_one_kernel(
    dir_ref, mine_ref, other_ref, phi_ref, theta_ref, shift_ref, out_ref, expand, near, far, phi4, rows_f32
):
    step = pl.program_id(0)
    dir_index = dir_ref[0]

    @pl.when(step == 0)
    def _():
        spread = (
            lax.broadcasted_iota(jnp.int32, (32, 2048), 0)
            == lax.broadcasted_iota(jnp.int32, (32, 2048), 1) // 64
        ).astype(F32).astype(BF16)
        expand[...] = lax.dot_general(
            theta_ref[...], spread, (((0,), (0,)), ((), ())), preferred_element_type=F32
        )
        phi4[...] = jnp.zeros_like(phi4)
        for s in range(4):
            phi4[64 * s : 64 * s + 64, 128 * s : 128 * s + 128] = phi_ref[...]

    diagonal = (
        lax.broadcasted_iota(jnp.int32, (64, 256), 0) == lax.broadcasted_iota(jnp.int32, (64, 256), 1) % 64
    )
    near_rows = pl.multiple_of(dir_index * 8, 8)
    far_rows = pl.multiple_of((1 - dir_index) * 8, 8)
    for part in range(4):
        lanes = pl.ds(pl.multiple_of(step * 1024 + part * 256, 256), 256)
        near_values = expand[pl.ds(near_rows, 8), lanes]
        far_values = expand[pl.ds(far_rows, 8), lanes]
        for t in range(8):
            near[64 * t : 64 * t + 64, :] = jnp.where(diagonal, near_values[t : t + 1], 0.0).astype(BF16)
            far[64 * t : 64 * t + 64, :] = jnp.where(diagonal, far_values[t : t + 1], 0.0).astype(BF16)
        theta_out = dot(mine_ref[...].reshape(512, 512), near[...]) + dot(
            other_ref[...].reshape(512, 512), far[...]
        )
        fine = dot(theta_out.astype(BF16), phi4[...])
        real_sum = jnp.zeros((32, 512), F32)
        imag_sum = jnp.zeros((32, 512), F32)
        for b in range(8):
            real_part = fine[64 * b : 64 * b + 32]
            imag_part = fine[64 * b + 32 : 64 * b + 64]
            factors = shift_ref[b, :, 512 * part : 512 * part + 512].astype(F32)
            f_real, f_imag = factors[0:1], factors[1:2]
            real_sum = real_sum + (real_part * f_real - imag_part * f_imag)
            imag_sum = imag_sum + (real_part * f_imag + imag_part * f_real)
        for s in range(4):
            rows_f32[0:32, 4 * part + s, :] = real_sum[:, 128 * s : 128 * s + 128]
            rows_f32[32:64, 4 * part + s, :] = imag_sum[:, 128 * s : 128 * s + 128]
    for d in range(8):
        out_ref[d, 0] = rows_f32[4 * d : 4 * d + 4].astype(BF16)
        out_ref[d, 1] = rows_f32[32 + 4 * d : 36 + 4 * d].astype(BF16)


def level_one_patterns(dir_index, leaf, received, phi, theta, shift):
    return pl.pallas_call(
        level_one_kernel,
        grid_spec=pltpu.PrefetchScalarGridSpec(
            num_scalar_prefetch=1,
            grid=(2,),
            in_specs=[
                pl.BlockSpec((8, 2, 32, 512), lambda i, d: (0, 0, 0, 0)),
                pl.BlockSpec((8, 2, 32, 512), lambda i, d: (0, 0, 0, 0)),
                pl.BlockSpec((64, 128), lambda i, d: (0, 0)),
                pl.BlockSpec((32, 16), lambda i, d: (0, 0)),
                pl.BlockSpec((8, 2, 2048), lambda i, d: (0, 0, i)),
            ],
            out_specs=pl.BlockSpec((8, 2, 4, 16, 128), lambda i, d: (0, 0, 0, i, 0)),
            scratch_shapes=[
                pltpu.VMEM((16, 2048), F32),
                pltpu.VMEM((512, 256), BF16),
                pltpu.VMEM((512, 256), BF16),
                pltpu.VMEM((256, 512), BF16),
                pltpu.VMEM((64, 16, 128), F32),
            ],
        ),
        out_shape=jax.ShapeDtypeStruct((8, 2, 4, 32, 128), BF16),
        compiler_params=params(24),
        cost_estimate=cost(1, 1),
        name="level_one",
    )(dir_index, leaf, received, phi, theta, shift)


def level_two_kernel(kids_ref, phi_ref, theta_ref, shift_ref, out_ref, blocks, total, turned):
    tiled = dot(
        theta_ref[...],
        (
            lax.broadcasted_iota(jnp.int32, (32, 256), 0)
            == lax.broadcasted_iota(jnp.int32, (32, 256), 1) % 32
        ).astype(F32).astype(BF16),
    )
    owner = lax.broadcasted_iota(jnp.int32, (64, 256), 1) // 32
    for m in range(8):
        blocks[64 * m : 64 * m + 64, :] = jnp.where(owner == m, tiled, 0.0).astype(BF16)
    total[...] = jnp.zeros_like(total)

    def child(o, carry):
        along_phi = dot(kids_ref[o].reshape(256, 128), phi_ref[...]).astype(BF16)
        along_theta = dot(blocks[...], along_phi)
        f_real = shift_ref[o, 0].astype(F32)
        f_imag = shift_ref[o, 1].astype(F32)
        for r in range(4):
            real_part = along_theta[64 * r : 64 * r + 64]
            imag_part = along_theta[256 + 64 * r : 320 + 64 * r]
            total[r] = total[r] + (real_part * f_real - imag_part * f_imag)
            total[4 + r] = total[4 + r] + (real_part * f_imag + imag_part * f_real)
        return carry

    lax.fori_loop(0, 8, child, 0)
    for m in range(8):
        turned[:, m, :] = total[m]
    out_ref[:, 0] = turned[:, :, 0:128].astype(BF16)
    out_ref[:, 1] = turned[:, :, 128:256].astype(BF16)


def level_two_terms(kids, phi, theta, shift):
    return pl.pallas_call(
        level_two_kernel,
        out_shape=jax.ShapeDtypeStruct((64, 2, 8, 128), BF16),
        in_specs=[pl.BlockSpec(memory_space=pltpu.VMEM)] * 4,
        out_specs=pl.BlockSpec(memory_space=pltpu.VMEM),
        scratch_shapes=[
            pltpu.VMEM((512, 256), BF16),
            pltpu.VMEM((8, 64, 256), F32),
            pltpu.VMEM((64, 8, 256), F32),
        ],
        compiler_params=params(16),
        cost_estimate=cost(1, 1),
        name="level_two",
    )(kids, phi, theta, shift)


def upper_operators_kernel(rel_ref, ops_ref, after_ref, out_ref):
    del after_ref
    for h in range(8):
        for i in range(4):
            out_ref[h, i] = ops_ref[rel_ref[h, i]].astype(F32)


def upper_operators(rel, operators, after):
    return pl.pallas_call(
        upper_operators_kernel,
        in_specs=[SMEM, VMEM, ANYWHERE],
        out_specs=VMEM,
        out_shape=jax.ShapeDtypeStruct((8, 4, 2, 128), F32),
        compiler_params=params(8),
        cost_estimate=cost(1 << 34, 1),
        name="upper_operators",
    )(rel, operators, after)


def upper_kernel(src_ref, got_ref, ops_ref, out_ref, plain, rolled):
    for h in range(8):
        for g in range(8):
            for d in range(2):
                tile = got_ref[h, g, d].astype(F32)
                plain[h, 2 * g + d] = tile
                rolled[h, 2 * g + d] = pltpu.roll(tile, 4, 0)
    low = lax.broadcasted_iota(jnp.int32, (8, 128), 0) < 4

    def one(h, carry):
        total = jnp.zeros((16, 8, 128), F32)
        for i in range(4):
            operator = ops_ref[h, i]
            op_real = jnp.broadcast_to(operator[0:1], (8, 128))
            op_imag = jnp.broadcast_to(operator[1:2], (8, 128))
            op_imag = jnp.where(low, -op_imag, op_imag)
            src = src_ref[h, i]
            total = total + (plain[src] * op_real[None] + rolled[src] * op_imag[None])
        for g in range(8):
            for d in range(2):
                start = 32 * d + 4 * g
                out_ref[h, 0, start : start + 4, :] = total[2 * g + d, 0:4]
                out_ref[h, 1, start : start + 4, :] = total[2 * g + d, 4:8]
        return carry

    lax.fori_loop(0, 8, one, 0)


def upper_translate(il2_src, got, operators):
    return pl.pallas_call(
        upper_kernel,
        out_shape=jax.ShapeDtypeStruct((8, 2, 64, 128), F32),
        in_specs=[SMEM, VMEM, VMEM],
        out_specs=VMEM,
        scratch_shapes=[pltpu.VMEM((8, 16, 8, 128), F32), pltpu.VMEM((8, 16, 8, 128), F32)],
        compiler_params=params(12),
        cost_estimate=cost(1 << 34, 1),
        name="upper_translate",
    )(il2_src, got, operators)


def near_kernel(
    link_ref,
    place_ref,
    blocks_hbm,
    own_hbm,
    one_hbm,
    one2_hbm,
    two_hbm,
    two2_hbm,
    out_hbm,
    blocks,
    boxes,
    result,
    self_sems,
    block_sems,
    box_sems,
    out_sems,
):
    mine = place_ref[0] * 4
    theirs = 4 - mine
    one = place_ref[1] * 16
    two = 16 - one

    def beside(source, start, sem):
        return pltpu.make_async_copy(source, boxes.at[pl.ds(pl.multiple_of(start, 4), 4)], box_sems.at[sem])

    def self_block(b):
        return pltpu.make_async_copy(blocks_hbm.at[b, 0], blocks.at[b, 0], self_sems.at[b])

    def other_blocks(b):
        rest = pl.ds(1, 2)
        return pltpu.make_async_copy(blocks_hbm.at[b, rest], blocks.at[b, rest], block_sems.at[b])

    own_copy = pltpu.make_async_copy(own_hbm, boxes.at[pl.ds(8, 8)], box_sems.at[4])
    own_copy.start()
    for b in range(8):
        self_block(b).start()
    copies = [
        beside(one_hbm, one + mine, 0),
        beside(one2_hbm, one + theirs, 1),
        beside(two_hbm, two + mine, 2),
        beside(two2_hbm, two + theirs, 3),
    ]
    for copy in copies:
        copy.start()
    for b in range(8):
        other_blocks(b).start()

    def product(b, j, box):
        rows = boxes[box].reshape(128, 512)
        first = dot_nt(rows, blocks[b, j, 0])
        second = dot_nt(rows, blocks[b, j, 1])
        return first[:64] - second[64:], second[:64] + first[64:]

    own_copy.wait()

    def itself(b, carry):
        self_block(b).wait()
        result[b, 0], result[b, 1] = product(b, 0, link_ref[b, 0])
        return carry

    lax.fori_loop(0, 8, itself, 0)
    for copy in copies:
        copy.wait()

    def others(b, carry):
        other_blocks(b).wait()
        real_one, imag_one = product(b, 1, link_ref[b, 1])
        real_two, imag_two = product(b, 2, link_ref[b, 2])
        result[b, 0] = result[b, 0] + (real_one + real_two)
        result[b, 1] = result[b, 1] + (imag_one + imag_two)
        pltpu.make_async_copy(result.at[b], out_hbm.at[b], out_sems.at[b]).start()
        return carry

    lax.fori_loop(0, 8, others, 0)
    for b in range(8):
        pltpu.make_async_copy(result.at[b], out_hbm.at[b], out_sems.at[b]).wait()


def near_products(links, places, near_blocks, own, one, one2, two, two2):
    return pl.pallas_call(
        near_kernel,
        in_specs=[SMEM, SMEM] + [HBM] * 6,
        out_specs=HBM,
        out_shape=jax.ShapeDtypeStruct((8, 2, 64, 256), F32),
        scratch_shapes=[
            pltpu.VMEM((8, 3, 2, 256, 512), BF16),
            pltpu.VMEM((24, 2, 64, 512), BF16),
            pltpu.VMEM((8, 2, 64, 256), F32),
            pltpu.SemaphoreType.DMA((8,)),
            pltpu.SemaphoreType.DMA((8,)),
            pltpu.SemaphoreType.DMA((5,)),
            pltpu.SemaphoreType.DMA((8,)),
        ],
        compiler_params=params(24),
        cost_estimate=cost(1 << 30, 1),
        name="near_field",
    )(links, places, in_hbm(near_blocks), in_hbm(own), one, one2, two, two2)


def gather_kernel(rel_ref, count_ref, ops_ref, after_ref, out_ref):
    del after_ref

    def box(b, carry):
        def entry(i, inner):
            out_ref[b, i] = ops_ref[rel_ref[b, i]].astype(F32)
            return inner

        lax.fori_loop(0, count_ref[b], entry, 0)
        return carry

    lax.fori_loop(0, 8, box, 0)


def gather_operators(rel, count, operators, after):
    return pl.pallas_call(
        gather_kernel,
        in_specs=[SMEM, SMEM, VMEM, ANYWHERE],
        out_specs=VMEM,
        out_shape=jax.ShapeDtypeStruct((8, 16, 2, 512), F32),
        compiler_params=params(8),
        cost_estimate=cost(1 << 20, 1),
        name="leaf_operators",
    )(rel, count, operators, after)


def links_kernel(src_ref, first_ref, after_ref, out_ref):
    del after_ref
    out_ref[...] = src_ref[...] - first_ref[0]


def link_offsets(src, first_box, after):
    return pl.pallas_call(
        links_kernel,
        in_specs=[VMEM, SMEM, ANYWHERE],
        out_specs=VMEM,
        out_shape=jax.ShapeDtypeStruct((8, 16), jnp.int32),
        compiler_params=params(4),
        cost_estimate=cost(1 << 34, 1),
        name="leaf_links",
    )(src, first_box, after)


def translate_kernel(
    first_row,
    place_ref,
    link_ref,
    count_ref,
    ops_ref,
    own_ref,
    one_ref,
    two_ref,
    *rest,
):
    out_hbm, boxes, wide, result, box_sems, out_sems = rest[-6:]
    one = pl.multiple_of(place_ref[1] * 16, 8)
    two = pl.multiple_of(16 - place_ref[1] * 16, 8)
    copies = [
        pltpu.make_async_copy(one_ref, boxes.at[pl.ds(one, 8)], box_sems.at[0]),
        pltpu.make_async_copy(own_ref, boxes.at[pl.ds(8, 8)], box_sems.at[1]),
        pltpu.make_async_copy(two_ref, boxes.at[pl.ds(two, 8)], box_sems.at[2]),
    ]
    for copy in copies:
        copy.start()

    def store(b):
        return pltpu.make_async_copy(
            result.at[b], out_hbm.at[b, :, pl.ds(first_row, 32), :], out_sems.at[b]
        )

    def box(b, carry):
        count = count_ref[b]

        def widen(i, inner):
            row = ops_ref[b, i]
            wide[i, 0] = jnp.broadcast_to(row[0:1], (16, 512)).astype(BF16)
            wide[i, 1] = jnp.broadcast_to(row[1:2], (16, 512)).astype(BF16)
            return inner

        lax.fori_loop(0, count, widen, 0)
        wide[count] = jnp.zeros((2, 16, 512), BF16)

        @pl.when(b == 0)
        def _():
            for copy in copies:
                copy.wait()

        def term(i):
            link = link_ref[b, jnp.minimum(i, 15)]
            real_part = boxes[link, 0].reshape(2, 16, 512)
            imag_part = boxes[link, 1].reshape(2, 16, 512)
            op_real = wide[i, 0][None]
            op_imag = wide[i, 1][None]
            return (
                op_real * real_part - op_imag * imag_part,
                op_real * imag_part + op_imag * real_part,
            )

        def pair(i, sums):
            real_one, imag_one = term(2 * i)
            real_two, imag_two = term(2 * i + 1)
            return (
                sums[0] + (real_one + real_two).reshape(32, 512).astype(F32),
                sums[1] + (imag_one + imag_two).reshape(32, 512).astype(F32),
            )

        zero = jnp.zeros((32, 512), F32)
        real_sum, imag_sum = lax.fori_loop(0, (count + 1) // 2, pair, (zero, zero))
        result[b, 0] = real_sum
        result[b, 1] = imag_sum
        store(b).start()
        return carry

    lax.fori_loop(0, 8, box, 0)
    for b in range(8):
        store(b).wait()


def leaf_translate(first_row, places, links, count, operators, own, one, two, partly=None):
    earlier = [] if partly is None else [partly]
    return pl.pallas_call(
        functools.partial(translate_kernel, first_row),
        in_specs=[SMEM] * 3 + [VMEM] + [ANYWHERE] * 3 + [HBM] * len(earlier),
        out_specs=HBM,
        out_shape=jax.ShapeDtypeStruct((8, 2, 64, 512), F32),
        scratch_shapes=[
            pltpu.VMEM((24, 2, 32, 512), BF16),
            pltpu.VMEM((18, 2, 16, 512), BF16),
            pltpu.VMEM((8, 2, 32, 512), F32),
            pltpu.SemaphoreType.DMA((3,)),
            pltpu.SemaphoreType.DMA((8,)),
        ],
        input_output_aliases={7: 0} if earlier else {},
        compiler_params=params(16),
        cost_estimate=cost(1 << 30, 1),
        name="leaf_translate",
    )(places, links, count, operators, own, one, two, *earlier)


def local(
    sources,
    near_blocks,
    near_src,
    radiation,
    il0_src,
    il0_rel,
    il0_count,
    trans0,
    phi_interp1,
    theta_interp1,
    shift1,
    phi_interp2,
    theta_interp2,
    shift2,
    il2_src,
    il2_rel,
    trans2,
):
    box_index = lax.axis_index(BOX)
    dir_position = lax.axis_index("dir")
    dir_index = dir_position.astype(jnp.int32).reshape(1)
    owners = lax.axis_size(BOX)
    first_box = (box_index - 1) * 8
    places = jnp.stack([dir_position, 1 - box_index % 2]).astype(jnp.int32)
    with_one = [(i, i ^ 1) for i in range(owners)]
    with_two = [(i, (i + 1 - 2 * ((i + 1) % 2)) % owners) for i in range(owners)]
    swap = [(0, 1), (1, 0)]

    half, send, low, high, mine = leaf_patterns(dir_index, sources, radiation)
    received = lax.ppermute(send, "dir", swap)
    two = lax.ppermute(half, BOX, with_two)
    one = lax.ppermute(half, BOX, with_one)
    two_swapped = lax.ppermute(two, "dir", swap)
    one_swapped = lax.ppermute(one, "dir", swap)
    mine, factors_two = lax.optimization_barrier((mine, shift2.reshape(8, 2, 64, 256)))
    level_one = level_one_patterns(dir_index, mine, received, phi_interp1, theta_interp1, shift1)

    kids = lax.all_to_all(level_one, ("xl", "z"), 0, 0, tiled=True)
    operators_two = upper_operators(il2_rel, trans2.reshape(316, 2, 128), level_one)
    low, near_links, operators_two = lax.optimization_barrier(
        (low, (near_src - first_box).astype(jnp.int32), operators_two)
    )
    low_two = lax.ppermute(low, BOX, with_two)
    low_one = lax.ppermute(low, BOX, with_one)
    near_field = near_products(near_links, places, near_blocks, sources, one, one_swapped, two, two_swapped)
    kids, near_field = lax.optimization_barrier((kids, near_field))
    terms = level_two_terms(kids, phi_interp2, theta_interp2, factors_two)

    got = lax.all_to_all(terms.reshape(128, 8, 128), ALL, 0, 0, tiled=True)
    links = link_offsets(il0_src, first_box.astype(jnp.int32).reshape(1), terms)
    high, links, rel = lax.optimization_barrier((high, links, il0_rel))
    high_two = lax.ppermute(high, BOX, with_two)
    high_one = lax.ppermute(high, BOX, with_one)
    operators = gather_operators(rel, il0_count, trans0, links)
    partly = leaf_translate(0, places, links, il0_count, operators, low, low_one, low_two)
    got, partly = lax.optimization_barrier((got, partly))
    upper = upper_translate(il2_src, got.reshape(8, 8, 2, 8, 128), operators_two)
    partly, upper = lax.optimization_barrier((partly, upper))
    leaf_incoming = leaf_translate(32, places, links, il0_count, operators, high, high_one, high_two, partly)
    return near_field, leaf_incoming, upper.reshape(8, 2, 64, 1, 128)


def solution(mesh):
    fine = Mesh(mesh.devices.reshape(4, 2, 2, 4, 2), ALL)
    placed = (
        P(BOX, None, None, None),
        P(BOX, None, None, "dir", None),
        P(BOX, None),
        P(BOX, None, None, "dir"),
        P(BOX, None),
        P(BOX, None),
        P(BOX),
        P(None, None, "dir"),
        P(),
        P(),
        P(),
        P(),
        P(),
        P(),
        P(),
        P(),
        P(None, None, BOX, "dir"),
    )
    return jax.shard_map(
        local,
        mesh=fine,
        in_specs=placed,
        out_specs=(
            P(BOX, None, None, "dir"),
            P(BOX, None, None, "dir"),
            P(None, None, None, BOX, "dir"),
        ),
        check_vma=False,
    )
```

time: 107 us -> 85.2 us (0.80)
  waiting for transfers between devices: 23.9 us -> 6.63 us
  starting transfers between devices: 25.9 us -> 33.4 us
  local copies, waits for them, and re-layouts: 9.21 us -> 3.08 us
  Pallas kernels: 45.9 us -> 40.8 us
    all_to_all x1, waiting for transfers between devices: 23.9 us -> 0.01 us  [local(): kids = lax.all_to_all(level_one, ('xl', 'z'), 0, 0, tiled=True)]
    ppermute x6 -> x8, starting transfers between devices: 16.3 us -> 24.3 us  [the longest x1 8.49 us: local(): two = lax.ppermute(half, BOX, with_two)]
    ppermute x6 -> x8, waiting for transfers between devices: 0.02 us -> 6.63 us  [the longest x1 6.61 us: local(): high_two = lax.ppermute(high, BOX, with_two)]
    unnamed x41 -> x35, local copies, waits for them, and re-layouts: 6.21 us -> 1.7 us
    pallas_call x3 -> x7, Pallas kernels: 30.8 us -> 26.6 us  [the longest x1 10.2 us: near_products(): pl.pallas_call(near_kernel, in_specs=[SMEM, SMEM] + [HBM] * 6, out_specs=...]
  transfers between devices with their start and end apart: 9 -> 11, of which waited for: 1 -> 1; matrix products, arithmetic and copies ran while one was open for 3% -> 2% of each run, Pallas kernels for 34% -> 36%
where the time goes in v2:
time: 85.2 us; the launch traced here: 84.9 us
  Pallas kernels  40.8 us (48%)
  starting transfers between devices  33.4 us (39%)
  waiting for transfers between devices  6.63 us (8%)
  local copies, waits for them, and re-layouts  3.08 us (4%)
  between operations  0.9 us (1%)
    pallas_call x1, Pallas kernels, near_products(): pl.pallas_call(near_kernel, in_specs=[SMEM, SMEM] + [HBM] * 6, out_specs=...  10.2 us
    ppermute x1, starting transfers between devices, local(): two = lax.ppermute(half, BOX, with_two)  8.49 us
    ppermute x1, starting transfers between devices, local(): high_two = lax.ppermute(high, BOX, with_two)  7.91 us
    pallas_call x1, Pallas kernels, level_one_patterns(): pl.pallas_call(level_one_kernel, grid_spec=pltpu.PrefetchScalarGridSpec(n...  7.85 us
    pallas_call x2, Pallas kernels, leaf_translate(): pl.pallas_call(functools.partial(translate_kernel, first_row), in_specs=[...  7.78 us
    pallas_call x1, Pallas kernels, leaf_patterns(): pl.pallas_call(leaf_kernel, in_specs=[SMEM, HBM, HBM], out_specs=[HBM, HB...  6.83 us
    ppermute x1, starting transfers between devices, local(): low_two = lax.ppermute(low, BOX, with_two)  6.62 us
    ppermute x1, waiting for transfers between devices, local(): high_two = lax.ppermute(high, BOX, with_two)  6.61 us
  transfers between devices with their start and end apart: 11, of which 1 were waited for; matrix products, arithmetic and copies ran while one was open for 2% of the time, Pallas kernels for 36%

profile of v2, /device:TPU:1, one launch (start us, length us, event | category | flops | bytes accessed | tf_op | source)
XLA Modules:
  0.0 84.9 jit_solution(14259182064107414013)
XLA Ops:
  0.6 0.0 copy-start.12
  0.6 0.0 copy-start.13
  0.7 0.0 copy-start.14
  0.7 0.0 copy-start.11
  0.7 0.0 copy-start.10
  0.7 0.0 copy-start.3
  0.7 0.0 copy-start.5
  0.7 0.0 copy-start.8
  0.7 6.8 %leaf_patterns.1 = (bf16[4,2,64,512]{3,2,1,0:T(8,128)(2,1)}, bf16[8,2,32,512]{3,2,1,0:T(8,128)(2,1)}, bf16[8,2,32,512]{3,2,1,0:T(8,128)(2,1)S(1)}, bf16[8,2,32,5...) custom-call(s32[1]{0:T(128)} %bitcast.dir_ref, bf16[8,2,64,512]{3,2,1,0:T(8,128)(2,1)} %own_hbm.1, ...), custom_call_target="tpu_custom_call" | custom-call | flops 1 | bytes 1 | tf_op jit(solution)/shard_map/leaf_patterns/pallas_call | solution.py:92
  7.6 0.0 copy-start.1
  7.6 0.8 copy-done.1
  8.4 1.4 %collective-permute-start = (bf16[8,2,32,512]{3,2,1,0:T(8,128)(2,1)}, bf16[8,2,32,512]{3,2,1,0:T(8,128)(2,1)S(1)}, u32[]{:S(2)}, u32[]{:S(2)}) collective-permute-start(bf16[8,2,32,512]{3,2,1,0:T(8,128)(2,1)} %get-tuple-element.24), channel_id=1, source_target_pairs={{0,1},{1,0},{2,3},{3,2},{4,5},{5,4},{6,7},{7,6},{8,9},{9,8},{10,11... | collective-permute-start | bytes 1572872 | tf_op jit(solution)/shard_map/ppermute | solution.py:572
  9.8 8.5 %collective-permute-start.3 = (bf16[4,2,64,512]{3,2,1,0:T(8,128)(2,1)}, bf16[4,2,64,512]{3,2,1,0:T(8,128)(2,1)S(1)}, u32[]{:S(2)}, u32[]{:S(2)}) collective-permute-start(bf16[4,2,64,512]{3,2,1,0:T(8,128)(2,1)} %get-tuple-element.27), channel_id=1, source_target_pairs={{0,126},{2,4},{4,2},{6,8},{8,6},{10,12},{12,10},{14,16},{16,14},{1... | collective-permute-start | bytes 1572872 | tf_op jit(solution)/shard_map/ppermute | solution.py:573
  18.3 0.0 collective-permute-start.1
  18.3 0.0 copy-done.12
  18.3 0.1 copy.22
  18.3 0.0 copy-done.13
  18.4 0.1 copy.25.src_ref
  18.4 0.0 copy-done.14
  18.4 0.1 copy.23.rel_ref
  18.5 0.0 copy-done.11
  18.5 0.1 copy.21.theta_ref
  18.6 0.0 copy-done.10
  18.6 0.1 copy.24.theta_ref
  18.7 1.4 %reshape.28.shift_ref = bf16[8,2,64,256]{3,2,1,0:T(8,128)(2,1)S(1)} reshape(bf16[8,2,16384]{2,1,0:T(2,128)(2,1)} %param.30) | data formatting | bytes 1048576 | tf_op jit(solution)/shard_map/reshape | solution.py:577
  20.1 0.1 pad_add_fusion.place_ref
  20.2 0.0 collective-permute-done.other_ref
  20.2 0.0 copy-done.3
  20.2 0.0 copy-done.5
  20.2 7.9 %level_one.1.after_ref = bf16[8,2,4,32,128]{4,3,2,1,0:T(8,128)(2,1)} custom-call(s32[1]{0:T(128)} %bitcast.dir_ref, bf16[8,2,32,512]{3,2,1,0:T(8,128)(2,1)S(1)} %get-tuple-element.23.mine_ref, bf16[8,2,32,512]{3,2,1,0:T(8,128)(2,1)S(1)} %collective-permute-done.other_ref, bf16[64,128]{1,0:T(8,128)(2,1)S(1)} %copy-done.5, bf16[32,16]{1,0:T(8,128)(2,1)S(1)} %copy.21.theta_ref, ...), custom_call_target="tpu_custom_call" | custom-call | flops 1 | bytes 1 | tf_op jit(solution)/shard_map/level_one/pallas_call | solution.py:166
  28.0 3.5 %all-to-all-start = ((bf16[8,2,4,32,128]{4,3,2,1,0:T(8,128)(2,1)}), bf16[8,2,4,32,128]{4,3,2,1,0:T(8,128)(2,1)S(1)}, u32[]{:S(2)}, u32[]{:S(2)}) async-start(bf16[8,2,4,32,128]{4,3,2,1,0:T(8,128)(2,1)} %level_one.1.after_ref), calls=%async_computation | async-start | bytes 1048576 | tf_op jit(solution)/shard_map/all_to_all | solution.py:580
  31.5 0.0 collective-permute-done.3.two_hbm
  31.6 0.4 collective-permute-start.4
  31.9 0.0 collective-permute-done.1.one_hbm
  31.9 0.9 %collective-permute-start.2 = (bf16[4,2,64,512]{3,2,1,0:T(8,128)(2,1)S(1)}, bf16[4,2,64,512]{3,2,1,0:T(8,128)(2,1)S(1)}, u32[]{:S(2)}, u32[]{:S(2)}) collective-permute-start(bf16[4,2,64,512]{3,2,1,0:T(8,128)(2,1)S(1)} %collective-permute-done.1.one_hbm), channel_id=1, source_target_pairs={{0,1},{1,0},{2,3},{3,2},{4,5},{5,4},{6,7},{7,6},{8,9},{9,8},{10,11... | collective-permute-start | bytes 1572872 | tf_op jit(solution)/shard_map/ppermute | solution.py:576
  32.8 0.0 copy-done.8
  32.8 0.6 upper_operators.1.ops_ref
  33.4 0.4 copy-done.2
  33.9 6.6 %collective-permute-start.8 = (bf16[8,2,32,512]{3,2,1,0:T(8,128)(2,1)S(1)}, bf16[8,2,32,512]{3,2,1,0:T(8,128)(2,1)}, u32[]{:S(2)}, u32[]{:S(2)}) collective-permute-start(bf16[8,2,32,512]{3,2,1,0:T(8,128)(2,1)S(1)} %copy-done.2), channel_id=1, source_target_pairs={{0,126},{2,4},{4,2},{6,8},{8,6},{10,12},{12,10},{14,16},{16,14},{1... | collective-permute-start | bytes 1572872 | tf_op jit(solution)/shard_map/ppermute | solution.py:585
  40.5 0.0 collective-permute-start.7
  40.5 0.0 collective-permute-done.4.two2_hbm
  40.5 0.0 collective-permute-done.2.one2_hbm
  40.5 10.2 %near_field.1 = f32[8,2,64,256]{3,2,1,0:T(8,128)} custom-call(s32[8,3]{1,0:T(8,128)S(1)} %broadcast_subtract_fusion.link_ref, s32[2]{0:T(128)S(1)} %pad_add_fusion.place_ref, bf16[8,3,2,256,512]{4,3,2,1,0:T(8,128)(2,1)} %blocks_hbm.1, bf16[8,2,64,512]{3,2,1,0:T(8,128)(2,1)} %own_hbm.1, bf16[4,2,64,512]{3,2,1,0:T(8,128)(2,1)S(1)} %collective-permute-done.1.one_hbm, ...), custom_call_target="tpu_custom_call" | custom-call | flops 1073741824 | bytes 1 | tf_op jit(solution)/shard_map/near_field/pallas_call | solution.py:383
  50.7 0.0 all-to-all-done.kids_ref
  50.7 0.0 copy-done.4
  50.7 4.5 %level_two.1.after_ref = bf16[64,2,8,128]{3,2,1,0:T(8,128)(2,1)} custom-call(bf16[8,2,4,32,128]{4,3,2,1,0:T(8,128)(2,1)S(1)} %all-to-all-done.kids_ref, bf16[128,256]{1,0:T(8,128)(2,1)S(1)} %copy-done.4, bf16[64,32]{1,0:T(8,128)(2,1)S(1)} %copy.24.theta_ref, bf16[8,2,64,256]{3,2,1,0:T(8,128)(2,1)S(1)} %reshape.28.shift_ref), custom_call_target="tpu_custom_call" | custom-call | flops 1 | bytes 1 | tf_op jit(solution)/shard_map/level_two/pallas_call | solution.py:227
  55.2 4.2 %all-to-all-start.1 = ((bf16[128,8,128]{2,1,0:T(8,128)(2,1)}), bf16[128,8,128]{2,1,0:T(8,128)(2,1)S(1)}, u32[]{:S(2)}, u32[]{:S(2)}) async-start(bf16[128,8,128]{2,1,0:T(8,128)(2,1)} %bitcast.4), calls=%async_computation.1 | async-start | bytes 524288 | tf_op jit(solution)/shard_map/all_to_all | solution.py:591
  59.4 0.0 copy-done.9
  59.4 0.0 copy-start
  59.5 0.0 copy-start.6
  59.5 0.0 copy-start.7
  59.5 7.9 %collective-permute-start.6 = (bf16[8,2,32,512]{3,2,1,0:T(8,128)(2,1)S(1)}, bf16[8,2,32,512]{3,2,1,0:T(8,128)(2,1)S(1)}, u32[]{:S(2)}, u32[]{:S(2)}) collective-permute-start(bf16[8,2,32,512]{3,2,1,0:T(8,128)(2,1)S(1)} %get-tuple-element.34.own_ref), channel_id=1, source_target_pairs={{0,126},{2,4},{4,2},{6,8},{8,6},{10,12},{12,10},{14,16},{16,14},{1... | collective-permute-start | bytes 1572872 | tf_op jit(solution)/shard_map/ppermute | solution.py:594
  67.4 0.0 collective-permute-start.5
  67.4 0.0 copy-done
  67.4 0.0 copy-done.6
  67.4 1.2 %leaf_operators.1.ops_ref = f32[8,16,2,512]{3,2,1,0:T(2,128)S(1)} custom-call(s32[8,16]{1,0:T(8,128)S(1)} %copy-done.7, s32[8]{0:T(128)S(1)} %copy-done.6, bf16[316,2,512]{2,1,0:T(2,128)(2,1)S(1)} %copy-done, s32[8,16]{1,0:T(8,128)S(1)} %leaf_links.1.after_ref.link_ref), custom_call_target="tpu_custom_call" | custom-call | flops 1048576 | bytes 1 | tf_op jit(solution)/shard_map/leaf_operators/pallas_call | solution.py:418
  68.6 0.0 collective-permute-done.8.two_ref
  68.6 0.0 collective-permute-done.7.one_ref
  68.6 4.4 %leaf_translate.2.rest_0_ = f32[8,2,64,512]{3,2,1,0:T(8,128)} custom-call(s32[2]{0:T(128)S(1)} %pad_add_fusion.place_ref, s32[8,16]{1,0:T(8,128)S(1)} %leaf_links.1.after_ref.link_ref, s32[8]{0:T(128)S(1)} %copy-done.6, f32[8,16,2,512]{3,2,1,0:T(2,128)S(1)} %leaf_operators.1.ops_ref, bf16[8,2,32,512]{3,2,1,0:T(8,128)(2,1)S(1)} %copy-done.2, ...), custom_call_target="tpu_custom_call" | custom-call | flops 1073741824 | bytes 1 | tf_op jit(solution)/shard_map/leaf_translate/pallas_call | solution.py:523
  73.1 0.0 all-to-all-done.1
  73.1 1.8 %upper_translate.1 = f32[8,2,64,128]{3,2,1,0:T(8,128)} custom-call(s32[8,4]{1,0:T(8,128)S(1)} %copy.25.src_ref, bf16[8,8,2,8,128]{4,3,2,1,0:T(8,128)(2,1)S(1)} %bitcast.9, f32[8,4,2,128]{3,2,1,0:T(2,128)S(1)} %upper_operators.1.ops_ref), custom_call_target="tpu_custom_call" | custom-call | flops 17179869184 | bytes 1 | tf_op jit(solution)/shard_map/upper_translate/pallas_call | solution.py:291
  74.9 6.6 %collective-permute-done.6.two_ref = bf16[8,2,32,512]{3,2,1,0:T(8,128)(2,1)S(1)} collective-permute-done((bf16[8,2,32,512]{3,2,1,0:T(8,128)(2,1)S(1)}, bf16[8,2,32,512]{3,2,1,0:T(8,128)(2,1)S(1)}, u32[]{:S(2)}, u32[]{:S(2)}) %collective-permute-start.6) | collective-permute-done | bytes 524320 | tf_op jit(solution)/shard_map/ppermute | solution.py:594
  81.5 0.0 collective-permute-done.5.one_ref
  81.5 3.4 %leaf_translate.3 = f32[8,2,64,512]{3,2,1,0:T(8,128)} custom-call(s32[2]{0:T(128)S(1)} %pad_add_fusion.place_ref, s32[8,16]{1,0:T(8,128)S(1)} %leaf_links.1.after_ref.link_ref, s32[8]{0:T(128)S(1)} %copy-done.6, f32[8,16,2,512]{3,2,1,0:T(2,128)S(1)} %leaf_operators.1.ops_ref, ...), custom_call_target="tpu_custom_call", output_to_operand_aliasing={{}: (7, {})} | custom-call | flops 1073741824 | bytes 1 | tf_op jit(solution)/shard_map/leaf_translate/pallas_call | solution.py:523
  (6 shorter events, 0.0 us)
Async XLA Ops:
  0.6 17.6 %copy-start.12 = (s32[8,3]{0,1:T(4,128)S(1)}, s32[8,3]{0,1:T(4,128)}, u32[]{:S(2)}) copy-start(s32[8,3]{0,1:T(4,128)} %param.19) | copy-start | bytes 292
  0.6 17.7 %copy-start.13 = (s32[8,4]{0,1:T(4,128)S(1)}, s32[8,4]{0,1:T(4,128)}, u32[]{:S(2)}) copy-start(s32[8,4]{0,1:T(4,128)} %param.31) | copy-start | bytes 388
  0.7 17.8 %copy-start.14 = (s32[8,4]{0,1:T(4,128)S(1)}, s32[8,4]{0,1:T(4,128)}, u32[]{:S(2)}) copy-start(s32[8,4]{0,1:T(4,128)} %param.32) | copy-start | bytes 388
  0.7 17.9 %copy-start.11 = (bf16[32,16]{0,1:T(8,128)(2,1)S(1)}, bf16[32,16]{0,1:T(8,128)(2,1)}, u32[]{:S(2)}) copy-start(bf16[32,16]{0,1:T(8,128)(2,1)} %param.26) | copy-start | bytes 3076
  0.7 17.9 %copy-start.10 = (bf16[64,32]{0,1:T(8,128)(2,1)S(1)}, bf16[64,32]{0,1:T(8,128)(2,1)}, u32[]{:S(2)}) copy-start(bf16[64,32]{0,1:T(8,128)(2,1)} %param.29) | copy-start | bytes 12292
  0.7 19.5 %copy-start.3 = (bf16[8,2,4096]{2,1,0:T(2,128)(2,1)S(1)}, bf16[8,2,4096]{2,1,0:T(2,128)(2,1)}, u32[]{:S(2)}) copy-start(bf16[8,2,4096]{2,1,0:T(2,128)(2,1)} %shift_ref.1) | copy-start | bytes 393220
  0.7 19.5 %copy-start.5 = (bf16[64,128]{1,0:T(8,128)(2,1)S(1)}, bf16[64,128]{1,0:T(8,128)(2,1)}, u32[]{:S(2)}) copy-start(bf16[64,128]{1,0:T(8,128)(2,1)} %phi_ref.2) | copy-start | bytes 49156
  0.7 32.1 %copy-start.8 = (bf16[316,2,1,128]{3,1,2,0:T(2,128)(2,1)S(1)}, bf16[316,2,1,128]{3,1,2,0:T(2,128)(2,1)}, u32[]{:S(2)}) copy-start(bf16[316,2,1,128]{3,1,2,0:T(2,128)(2,1)} %param.33) | copy-start | bytes 485380
  7.6 0.8 copy-start.1
  8.4 11.8 %collective-permute-start = (bf16[8,2,32,512]{3,2,1,0:T(8,128)(2,1)}, bf16[8,2,32,512]{3,2,1,0:T(8,128)(2,1)S(1)}, u32[]{:S(2)}, u32[]{:S(2)}) collective-permute-start(bf16[8,2,32,512]{3,2,1,0:T(8,128)(2,1)} %get-tuple-element.24), channel_id=1, source_target_pairs={{0,1},{1,0},{2,3},{3,2},{4,5},{5,4},{6,7},{7,6},{8,9},{9,8},{10,11... | collective-permute-start | bytes 1572872 | tf_op jit(solution)/shard_map/ppermute | solution.py:572
  9.8 21.8 %collective-permute-start.3 = (bf16[4,2,64,512]{3,2,1,0:T(8,128)(2,1)}, bf16[4,2,64,512]{3,2,1,0:T(8,128)(2,1)S(1)}, u32[]{:S(2)}, u32[]{:S(2)}) collective-permute-start(bf16[4,2,64,512]{3,2,1,0:T(8,128)(2,1)} %get-tuple-element.27), channel_id=1, source_target_pairs={{0,126},{2,4},{4,2},{6,8},{8,6},{10,12},{12,10},{14,16},{16,14},{1... | collective-permute-start | bytes 1572872 | tf_op jit(solution)/shard_map/ppermute | solution.py:573
  18.3 13.7 %collective-permute-start.1 = (bf16[4,2,64,512]{3,2,1,0:T(8,128)(2,1)}, bf16[4,2,64,512]{3,2,1,0:T(8,128)(2,1)S(1)}, u32[]{:S(2)}, u32[]{:S(2)}) collective-permute-start(bf16[4,2,64,512]{3,2,1,0:T(8,128)(2,1)} %get-tuple-element.27), channel_id=1, source_target_pairs={{0,2},{2,0},{4,6},{6,4},{8,10},{10,8},{12,14},{14,12},{16,18},{18,... | collective-permute-start | bytes 1572872 | tf_op jit(solution)/shard_map/ppermute | solution.py:574
  28.0 22.6 %all-to-all-start = ((bf16[8,2,4,32,128]{4,3,2,1,0:T(8,128)(2,1)}), bf16[8,2,4,32,128]{4,3,2,1,0:T(8,128)(2,1)S(1)}, u32[]{:S(2)}, u32[]{:S(2)}) async-start(bf16[8,2,4,32,128]{4,3,2,1,0:T(8,128)(2,1)} %level_one.1.after_ref), calls=%async_computation | async-start | bytes 1048576 | tf_op jit(solution)/shard_map/all_to_all | solution.py:580
  31.6 8.9 %collective-permute-start.4 = (bf16[4,2,64,512]{3,2,1,0:T(8,128)(2,1)S(1)}, bf16[4,2,64,512]{3,2,1,0:T(8,128)(2,1)S(1)}, u32[]{:S(2)}, u32[]{:S(2)}) collective-permute-start(bf16[4,2,64,512]{3,2,1,0:T(8,128)(2,1)S(1)} %collective-permute-done.3.two_hbm), channel_id=1, source_target_pairs={{0,1},{1,0},{2,3},{3,2},{4,5},{5,4},{6,7},{7,6},{8,9},{9,8},{10,11... | collective-permute-start | bytes 1572872 | tf_op jit(solution)/shard_map/ppermute | solution.py:575
  31.9 8.6 %collective-permute-start.2 = (bf16[4,2,64,512]{3,2,1,0:T(8,128)(2,1)S(1)}, bf16[4,2,64,512]{3,2,1,0:T(8,128)(2,1)S(1)}, u32[]{:S(2)}, u32[]{:S(2)}) collective-permute-start(bf16[4,2,64,512]{3,2,1,0:T(8,128)(2,1)S(1)} %collective-permute-done.1.one_hbm), channel_id=1, source_target_pairs={{0,1},{1,0},{2,3},{3,2},{4,5},{5,4},{6,7},{7,6},{8,9},{9,8},{10,11... | collective-permute-start | bytes 1572872 | tf_op jit(solution)/shard_map/ppermute | solution.py:576
  32.8 1.0 %copy-start.2 = (bf16[8,2,32,512]{3,2,1,0:T(8,128)(2,1)S(1)}, bf16[8,2,32,512]{3,2,1,0:T(8,128)(2,1)}, u32[]{:S(2)}) copy-start(bf16[8,2,32,512]{3,2,1,0:T(8,128)(2,1)} %copy-done.1) | copy-start | bytes 1572868
  33.9 16.8 %copy-start.4 = (bf16[128,256]{1,0:T(8,128)(2,1)S(1)}, bf16[128,256]{1,0:T(8,128)(2,1)}, u32[]{:S(2)}) copy-start(bf16[128,256]{1,0:T(8,128)(2,1)} %phi_ref.3) | copy-start | bytes 196612
  33.9 25.6 %copy-start.9 = (s32[8,16]{1,0:T(8,128)S(1)}, s32[8,16]{1,0:T(8,128)}, u32[]{:S(2)}) copy-start(s32[8,16]{1,0:T(8,128)} %src_ref.2) | copy-start | bytes 1540
  33.9 34.8 %collective-permute-start.8 = (bf16[8,2,32,512]{3,2,1,0:T(8,128)(2,1)S(1)}, bf16[8,2,32,512]{3,2,1,0:T(8,128)(2,1)}, u32[]{:S(2)}, u32[]{:S(2)}) collective-permute-start(bf16[8,2,32,512]{3,2,1,0:T(8,128)(2,1)S(1)} %copy-done.2), channel_id=1, source_target_pairs={{0,126},{2,4},{4,2},{6,8},{8,6},{10,12},{12,10},{14,16},{16,14},{1... | collective-permute-start | bytes 1572872 | tf_op jit(solution)/shard_map/ppermute | solution.py:585
  40.5 28.2 %collective-permute-start.7 = (bf16[8,2,32,512]{3,2,1,0:T(8,128)(2,1)S(1)}, bf16[8,2,32,512]{3,2,1,0:T(8,128)(2,1)}, u32[]{:S(2)}, u32[]{:S(2)}) collective-permute-start(bf16[8,2,32,512]{3,2,1,0:T(8,128)(2,1)S(1)} %copy-done.2), channel_id=1, source_target_pairs={{0,2},{2,0},{4,6},{6,4},{8,10},{10,8},{12,14},{14,12},{16,18},{18,... | collective-permute-start | bytes 1572872 | tf_op jit(solution)/shard_map/ppermute | solution.py:586
  55.2 17.9 %all-to-all-start.1 = ((bf16[128,8,128]{2,1,0:T(8,128)(2,1)}), bf16[128,8,128]{2,1,0:T(8,128)(2,1)S(1)}, u32[]{:S(2)}, u32[]{:S(2)}) async-start(bf16[128,8,128]{2,1,0:T(8,128)(2,1)} %bitcast.4), calls=%async_computation.1 | async-start | bytes 524288 | tf_op jit(solution)/shard_map/all_to_all | solution.py:591
  59.4 8.0 %copy-start = (bf16[316,2,512]{2,1,0:T(2,128)(2,1)S(1)}, bf16[316,2,512]{2,1,0:T(2,128)(2,1)}, u32[]{:S(2)}) copy-start(bf16[316,2,512]{2,1,0:T(2,128)(2,1)} %ops_ref.1) | copy-start | bytes 1941508
  59.5 8.0 %copy-start.6 = (s32[8]{0:T(128)S(1)}, s32[8]{0:T(128)}, u32[]{:S(2)}) copy-start(s32[8]{0:T(128)} %count_ref.5) | copy-start | bytes 100
  59.5 7.9 %copy-start.7 = (s32[8,16]{1,0:T(8,128)S(1)}, s32[8,16]{1,0:T(8,128)}, u32[]{:S(2)}) copy-start(s32[8,16]{1,0:T(8,128)} %rel_ref.1) | copy-start | bytes 1540
  59.5 22.0 %collective-permute-start.6 = (bf16[8,2,32,512]{3,2,1,0:T(8,128)(2,1)S(1)}, bf16[8,2,32,512]{3,2,1,0:T(8,128)(2,1)S(1)}, u32[]{:S(2)}, u32[]{:S(2)}) collective-permute-start(bf16[8,2,32,512]{3,2,1,0:T(8,128)(2,1)S(1)} %get-tuple-element.34.own_ref), channel_id=1, source_target_pairs={{0,126},{2,4},{4,2},{6,8},{8,6},{10,12},{12,10},{14,16},{16,14},{1... | collective-permute-start | bytes 1572872 | tf_op jit(solution)/shard_map/ppermute | solution.py:594
  67.4 14.1 %collective-permute-start.5 = (bf16[8,2,32,512]{3,2,1,0:T(8,128)(2,1)S(1)}, bf16[8,2,32,512]{3,2,1,0:T(8,128)(2,1)S(1)}, u32[]{:S(2)}, u32[]{:S(2)}) collective-permute-start(bf16[8,2,32,512]{3,2,1,0:T(8,128)(2,1)S(1)} %get-tuple-element.34.own_ref), channel_id=1, source_target_pairs={{0,2},{2,0},{4,6},{6,4},{8,10},{10,8},{12,14},{14,12},{16,18},{18,... | collective-permute-start | bytes 1572872 | tf_op jit(solution)/shard_map/ppermute | solution.py:595

commit v3 on v2

--- a/solution.py
+++ b/solution.py
@@ -1,5 +1,3 @@
-import functools
-
 import jax
 import jax.numpy as jnp
 from jax import lax
@@ -44,12 +42,10 @@
     rad_hbm,
     half_hbm,
     send_hbm,
-    low_ref,
-    high_ref,
+    leaf,
     mine_ref,
     src,
     rad,
-    leaf,
     src_sem,
     half_sem,
     rad_sems,
@@ -77,8 +73,6 @@
         leaf[b, 0] = (first[:64] - second[64:]).astype(BF16)
         leaf[b, 1] = (second[:64] + first[64:]).astype(BF16)
         send(b).start()
-        low_ref[b] = leaf[b, :, :32, :]
-        high_ref[b] = leaf[b, :, 32:, :]
         mine_ref[b] = leaf[b, :, pl.ds(mine, 32), :]
         return carry
 
@@ -92,13 +86,16 @@
     return pl.pallas_call(
         leaf_kernel,
         in_specs=[SMEM, HBM, HBM],
-        out_specs=[HBM, HBM, VMEM, VMEM, VMEM],
-        out_shape=[jax.ShapeDtypeStruct((4, 2, 64, 512), BF16)]
-        + [jax.ShapeDtypeStruct((8, 2, 32, 512), BF16)] * 4,
+        out_specs=[HBM, HBM, VMEM, VMEM],
+        out_shape=[
+            pltpu.HBM((4, 2, 64, 512), BF16),
+            pltpu.HBM((8, 2, 32, 512), BF16),
+            jax.ShapeDtypeStruct((8, 2, 64, 512), BF16),
+            jax.ShapeDtypeStruct((8, 2, 32, 512), BF16),
+        ],
         scratch_shapes=[
             pltpu.VMEM((8, 2, 64, 512), BF16),
             pltpu.VMEM((8, 2, 512, 512), BF16),
-            pltpu.VMEM((8, 2, 64, 512), BF16),
             pltpu.SemaphoreType.DMA,
             pltpu.SemaphoreType.DMA,
             pltpu.SemaphoreType.DMA((8,)),
@@ -444,7 +441,6 @@
 
 
 def translate_kernel(
-    first_row,
     place_ref,
     link_ref,
     count_ref,
@@ -452,9 +448,13 @@
     own_ref,
     one_ref,
     two_ref,
-    *rest,
+    out_hbm,
+    boxes,
+    wide,
+    result,
+    box_sems,
+    out_sems,
 ):
-    out_hbm, boxes, wide, result, box_sems, out_sems = rest[-6:]
     one = pl.multiple_of(place_ref[1] * 16, 8)
     two = pl.multiple_of(16 - place_ref[1] * 16, 8)
     copies = [
@@ -466,9 +466,7 @@
         copy.start()
 
     def store(b):
-        return pltpu.make_async_copy(
-            result.at[b], out_hbm.at[b, :, pl.ds(first_row, 32), :], out_sems.at[b]
-        )
+        return pltpu.make_async_copy(result.at[b], out_hbm.at[b], out_sems.at[b])
 
     def box(b, carry):
         count = count_ref[b]
@@ -487,29 +485,33 @@
             for copy in copies:
                 copy.wait()
 
-        def term(i):
-            link = link_ref[b, jnp.minimum(i, 15)]
-            real_part = boxes[link, 0].reshape(2, 16, 512)
-            imag_part = boxes[link, 1].reshape(2, 16, 512)
-            op_real = wide[i, 0][None]
-            op_imag = wide[i, 1][None]
-            return (
-                op_real * real_part - op_imag * imag_part,
-                op_real * imag_part + op_imag * real_part,
-            )
-
-        def pair(i, sums):
-            real_one, imag_one = term(2 * i)
-            real_two, imag_two = term(2 * i + 1)
-            return (
-                sums[0] + (real_one + real_two).reshape(32, 512).astype(F32),
-                sums[1] + (imag_one + imag_two).reshape(32, 512).astype(F32),
-            )
-
-        zero = jnp.zeros((32, 512), F32)
-        real_sum, imag_sum = lax.fori_loop(0, (count + 1) // 2, pair, (zero, zero))
-        result[b, 0] = real_sum
-        result[b, 1] = imag_sum
+        for start in range(0, 64, 32):
+            size = 32
+            chunk = slice(start, start + size)
+
+            def term(i):
+                link = link_ref[b, jnp.minimum(i, 15)]
+                real_part = boxes[link, 0, chunk, :].reshape(size // 16, 16, 512)
+                imag_part = boxes[link, 1, chunk, :].reshape(size // 16, 16, 512)
+                op_real = wide[i, 0][None]
+                op_imag = wide[i, 1][None]
+                return (
+                    op_real * real_part - op_imag * imag_part,
+                    op_real * imag_part + op_imag * real_part,
+                )
+
+            def pair(i, sums):
+                real_one, imag_one = term(2 * i)
+                real_two, imag_two = term(2 * i + 1)
+                return (
+                    sums[0] + (real_one + real_two).reshape(size, 512).astype(F32),
+                    sums[1] + (imag_one + imag_two).reshape(size, 512).astype(F32),
+                )
+
+            zero = jnp.zeros((size, 512), F32)
+            real_sum, imag_sum = lax.fori_loop(0, (count + 1) // 2, pair, (zero, zero))
+            result[b, 0, chunk, :] = real_sum
+            result[b, 1, chunk, :] = imag_sum
         store(b).start()
         return carry
 
@@ -518,25 +520,23 @@
         store(b).wait()
 
 
-def leaf_translate(first_row, places, links, count, operators, own, one, two, partly=None):
-    earlier = [] if partly is None else [partly]
-    return pl.pallas_call(
-        functools.partial(translate_kernel, first_row),
-        in_specs=[SMEM] * 3 + [VMEM] + [ANYWHERE] * 3 + [HBM] * len(earlier),
+def leaf_translate(places, links, count, operators, own, one, two):
+    return pl.pallas_call(
+        translate_kernel,
+        in_specs=[SMEM] * 3 + [VMEM] + [ANYWHERE] * 3,
         out_specs=HBM,
         out_shape=jax.ShapeDtypeStruct((8, 2, 64, 512), F32),
         scratch_shapes=[
-            pltpu.VMEM((24, 2, 32, 512), BF16),
+            pltpu.VMEM((24, 2, 64, 512), BF16),
             pltpu.VMEM((18, 2, 16, 512), BF16),
-            pltpu.VMEM((8, 2, 32, 512), F32),
+            pltpu.VMEM((8, 2, 64, 512), F32),
             pltpu.SemaphoreType.DMA((3,)),
             pltpu.SemaphoreType.DMA((8,)),
         ],
-        input_output_aliases={7: 0} if earlier else {},
         compiler_params=params(16),
         cost_estimate=cost(1 << 30, 1),
         name="leaf_translate",
-    )(places, links, count, operators, own, one, two, *earlier)
+    )(places, links, count, operators, own, one, two)
 
 
 def local(
@@ -565,10 +565,10 @@
     first_box = (box_index - 1) * 8
     places = jnp.stack([dir_position, 1 - box_index % 2]).astype(jnp.int32)
     with_one = [(i, i ^ 1) for i in range(owners)]
-    with_two = [(i, (i + 1 - 2 * ((i + 1) % 2)) % owners) for i in range(owners)]
+    with_two = [(i, i + 1 - 2 * ((i + 1) % 2)) for i in range(1, owners - 1)]
     swap = [(0, 1), (1, 0)]
 
-    half, send, low, high, mine = leaf_patterns(dir_index, sources, radiation)
+    half, send, leaf, mine = leaf_patterns(dir_index, sources, radiation)
     received = lax.ppermute(send, "dir", swap)
     two = lax.ppermute(half, BOX, with_two)
     one = lax.ppermute(half, BOX, with_one)
@@ -579,26 +579,21 @@
 
     kids = lax.all_to_all(level_one, ("xl", "z"), 0, 0, tiled=True)
     operators_two = upper_operators(il2_rel, trans2.reshape(316, 2, 128), level_one)
-    low, near_links, operators_two = lax.optimization_barrier(
-        (low, (near_src - first_box).astype(jnp.int32), operators_two)
+    leaf, near_links, operators_two = lax.optimization_barrier(
+        (leaf, (near_src - first_box).astype(jnp.int32), operators_two)
     )
-    low_two = lax.ppermute(low, BOX, with_two)
-    low_one = lax.ppermute(low, BOX, with_one)
+    leaf_two = lax.ppermute(leaf, BOX, with_two)
+    leaf_one = lax.ppermute(leaf, BOX, with_one)
     near_field = near_products(near_links, places, near_blocks, sources, one, one_swapped, two, two_swapped)
     kids, near_field = lax.optimization_barrier((kids, near_field))
     terms = level_two_terms(kids, phi_interp2, theta_interp2, factors_two)
 
     got = lax.all_to_all(terms.reshape(128, 8, 128), ALL, 0, 0, tiled=True)
     links = link_offsets(il0_src, first_box.astype(jnp.int32).reshape(1), terms)
-    high, links, rel = lax.optimization_barrier((high, links, il0_rel))
-    high_two = lax.ppermute(high, BOX, with_two)
-    high_one = lax.ppermute(high, BOX, with_one)
-    operators = gather_operators(rel, il0_count, trans0, links)
-    partly = leaf_translate(0, places, links, il0_count, operators, low, low_one, low_two)
-    got, partly = lax.optimization_barrier((got, partly))
+    operators = gather_operators(il0_rel, il0_count, trans0, links)
+    leaf_incoming = leaf_translate(places, links, il0_count, operators, leaf, leaf_one, leaf_two)
+    got, leaf_incoming = lax.optimization_barrier((got, leaf_incoming))
     upper = upper_translate(il2_src, got.reshape(8, 8, 2, 8, 128), operators_two)
-    partly, upper = lax.optimization_barrier((partly, upper))
-    leaf_incoming = leaf_translate(32, places, links, il0_count, operators, high, high_one, high_two, partly)
     return near_field, leaf_incoming, upper.reshape(8, 2, 64, 1, 128)
 
 

time: 85.2 us -> 74.3 us (0.87); the launches traced: 84.9 us -> 72.9 us
  starting transfers between devices: 33.4 us -> 28.7 us
  waiting for transfers between devices: 6.63 us -> 2.03 us
  Pallas kernels: 40.8 us -> 39.3 us
  local copies, waits for them, and re-layouts: 3.08 us -> 1.86 us
    ppermute x4 -> x2, starting transfers between devices: 14.5 us -> 3.39 us  [the longest x1 1.73 us: local(): leaf_one = lax.ppermute(leaf, BOX, with_one)]
    all_to_all x1, starting transfers between devices: 4.23 us -> 13.2 us  [local(): got = lax.all_to_all(terms.reshape(128, 8, 128), ALL, 0, 0, tiled=True)]
    ppermute x1, starting transfers between devices: 8.49 us -> 1.46 us  [local(): two = lax.ppermute(half, BOX, with_two)]
    ppermute x4 -> x2, waiting for transfers between devices: 6.62 us -> 0.01 us  [the longest x1 0.01 us: local(): leaf_one = lax.ppermute(leaf, BOX, with_one)]
    all_to_all x1, starting transfers between devices: 3.49 us -> 6.28 us  [local(): kids = lax.all_to_all(level_one, ('xl', 'z'), 0, 0, tiled=True)]
    all_to_all x1, waiting for transfers between devices: 0.01 us -> 2.01 us  [local(): got = lax.all_to_all(terms.reshape(128, 8, 128), ALL, 0, 0, tiled=True)]
    ppermute x1, starting transfers between devices: 0.01 us -> 1.73 us  [local(): one = lax.ppermute(half, BOX, with_one)]
    pallas_call x2 -> x1, Pallas kernels: 7.78 us -> 6.44 us  [leaf_translate(): pl.pallas_call(translate_kernel, in_specs=[SMEM] * 3 + [VMEM] + [ANYWHERE...]
  transfers between devices with their start and end apart: 11 -> 9, of which waited for: 1 -> 1; matrix products, arithmetic and copies ran while one was open for 2% -> 1% of each run, Pallas kernels for 36% -> 42%
where the time goes in v3:
time: 74.3 us; the launch traced here: 72.9 us
  Pallas kernels  39.3 us (53%)
  starting transfers between devices  28.7 us (39%)
  waiting for transfers between devices  2.03 us (3%)
  local copies, waits for them, and re-layouts  1.86 us (3%)
  between operations  0.9 us (1%)
    all_to_all x1, starting transfers between devices, local(): got = lax.all_to_all(terms.reshape(128, 8, 128), ALL, 0, 0, tiled=True)  13.2 us
    pallas_call x1, Pallas kernels, near_products(): pl.pallas_call(near_kernel, in_specs=[SMEM, SMEM] + [HBM] * 6, out_specs=...  10 us
    pallas_call x1, Pallas kernels, level_one_patterns(): pl.pallas_call(level_one_kernel, grid_spec=pltpu.PrefetchScalarGridSpec(n...  7.85 us
    pallas_call x1, Pallas kernels, leaf_patterns(): pl.pallas_call(leaf_kernel, in_specs=[SMEM, HBM, HBM], out_specs=[HBM, HB...  6.79 us
    pallas_call x1, Pallas kernels, leaf_translate(): pl.pallas_call(translate_kernel, in_specs=[SMEM] * 3 + [VMEM] + [ANYWHERE...  6.44 us
    all_to_all x1, starting transfers between devices, local(): kids = lax.all_to_all(level_one, ('xl', 'z'), 0, 0, tiled=True)  6.28 us
    pallas_call x1, Pallas kernels, level_two_terms(): pl.pallas_call(level_two_kernel, out_shape=jax.ShapeDtypeStruct((64, 2, 8...  4.5 us
    all_to_all x1, waiting for transfers between devices, local(): got = lax.all_to_all(terms.reshape(128, 8, 128), ALL, 0, 0, tiled=True)  2.01 us
  transfers between devices with their start and end apart: 9, of which 1 were waited for; matrix products, arithmetic and copies ran while one was open for 1% of the time, Pallas kernels for 42%

profile of v3, /device:TPU:1, one launch (start us, length us, event | category | flops | bytes accessed | tf_op | source)
XLA Modules:
  0.0 72.9 jit_solution(13561795969624914261)
XLA Ops:
  0.6 0.0 copy-start.8
  0.6 0.0 copy-start.10
  0.7 0.0 copy-start.11
  0.7 0.0 copy-start.12
  0.7 0.0 copy-start.9
  0.7 0.0 copy-start.13
  0.7 0.0 copy-start.3
  0.7 0.0 copy-start.1
  0.7 0.0 copy-start.6
  0.7 6.8 %leaf_patterns.1 = (bf16[4,2,64,512]{3,2,1,0:T(8,128)(2,1)}, bf16[8,2,32,512]{3,2,1,0:T(8,128)(2,1)}, bf16[8,2,64,512]{3,2,1,0:T(8,128)(2,1)S(1)}, bf16[8,2,32,512]{3,2,1,0:T(8,128)(2,1)S(1)}) custom-call(s32[1]{0:T(128)} %bitcast.dir_ref, bf16[8,2,64,512]{3,2,1,0:T(8,128)(2,1)} %own_hbm.1, bf16[8,2,512,512]{3,2,1,0:T(8,128)(2,1)} %rad_hbm.1), custom_call_target="tpu_custom_call" | custom-call | flops 1 | bytes 1 | tf_op jit(solution)/shard_map/leaf_patterns/pallas_call | solution.py:86
  7.5 1.5 %collective-permute-start = (bf16[8,2,32,512]{3,2,1,0:T(8,128)(2,1)}, bf16[8,2,32,512]{3,2,1,0:T(8,128)(2,1)S(1)}, u32[]{:S(2)}, u32[]{:S(2)}) collective-permute-start(bf16[8,2,32,512]{3,2,1,0:T(8,128)(2,1)} %get-tuple-element.18), channel_id=1, source_target_pairs={{0,1},{1,0},{2,3},{3,2},{4,5},{5,4},{6,7},{7,6},{8,9},{9,8},{10,11... | collective-permute-start | bytes 1572872 | tf_op jit(solution)/shard_map/ppermute | solution.py:572
  9.0 1.7 %collective-permute-start.1 = (bf16[4,2,64,512]{3,2,1,0:T(8,128)(2,1)}, bf16[4,2,64,512]{3,2,1,0:T(8,128)(2,1)}, u32[]{:S(2)}, u32[]{:S(2)}) collective-permute-start(bf16[4,2,64,512]{3,2,1,0:T(8,128)(2,1)} %get-tuple-element.21), channel_id=1, source_target_pairs={{0,2},{2,0},{4,6},{6,4},{8,10},{10,8},{12,14},{14,12},{16,18},{18,... | collective-permute-start | bytes 1572872 | tf_op jit(solution)/shard_map/ppermute | solution.py:574
  10.8 1.5 %collective-permute-start.3 = (bf16[4,2,64,512]{3,2,1,0:T(8,128)(2,1)}, bf16[4,2,64,512]{3,2,1,0:T(8,128)(2,1)}, u32[]{:S(2)}, u32[]{:S(2)}) collective-permute-start(bf16[4,2,64,512]{3,2,1,0:T(8,128)(2,1)} %get-tuple-element.21), channel_id=1, source_target_pairs={{2,4},{4,2},{6,8},{8,6},{10,12},{12,10},{14,16},{16,14},{18,20},{2... | collective-permute-start | bytes 1572872 | tf_op jit(solution)/shard_map/ppermute | solution.py:573
  12.2 0.0 copy-done.8
  12.2 0.3 reshape.28.shift_ref
  12.6 0.0 copy-done.10
  12.6 0.1 copy.20.theta_ref
  12.7 0.0 copy-done.11
  12.7 0.1 copy.21
  12.7 0.0 copy-done.12
  12.7 0.1 copy.22.rel_ref
  12.8 0.0 copy-done.9
  12.8 0.1 copy.23.theta_ref
  12.9 0.0 copy-done.13
  12.9 0.1 copy.24.src_ref
  13.0 0.1 pad_add_fusion.place_ref
  13.1 0.0 collective-permute-done.other_ref
  13.1 0.0 copy-done.3
  13.1 0.0 copy-done.1
  13.1 7.9 %level_one.1.after_ref = bf16[8,2,4,32,128]{4,3,2,1,0:T(8,128)(2,1)} custom-call(s32[1]{0:T(128)} %bitcast.dir_ref, bf16[8,2,32,512]{3,2,1,0:T(8,128)(2,1)S(1)} %get-tuple-element.17.mine_ref, bf16[8,2,32,512]{3,2,1,0:T(8,128)(2,1)S(1)} %collective-permute-done.other_ref, bf16[64,128]{1,0:T(8,128)(2,1)S(1)} %copy-done.3, bf16[32,16]{1,0:T(8,128)(2,1)S(1)} %copy.20.theta_ref, ...), custom_call_target="tpu_custom_call" | custom-call | flops 1 | bytes 1 | tf_op jit(solution)/shard_map/level_one/pallas_call | solution.py:163
  21.0 6.3 %all-to-all-start = ((bf16[8,2,4,32,128]{4,3,2,1,0:T(8,128)(2,1)}), bf16[8,2,4,32,128]{4,3,2,1,0:T(8,128)(2,1)S(1)}, u32[]{:S(2)}, u32[]{:S(2)}) async-start(bf16[8,2,4,32,128]{4,3,2,1,0:T(8,128)(2,1)} %level_one.1.after_ref), calls=%async_computation | async-start | bytes 1048576 | tf_op jit(solution)/shard_map/all_to_all | solution.py:580
  27.2 0.0 collective-permute-done.1.one_hbm
  27.3 1.0 %collective-permute-start.2 = (bf16[4,2,64,512]{3,2,1,0:T(8,128)(2,1)}, bf16[4,2,64,512]{3,2,1,0:T(8,128)(2,1)S(1)}, u32[]{:S(2)}, u32[]{:S(2)}) collective-permute-start(bf16[4,2,64,512]{3,2,1,0:T(8,128)(2,1)} %collective-permute-done.1.one_hbm), channel_id=1, source_target_pairs={{0,1},{1,0},{2,3},{3,2},{4,5},{5,4},{6,7},{7,6},{8,9},{9,8},{10,11... | collective-permute-start | bytes 1572872 | tf_op jit(solution)/shard_map/ppermute | solution.py:576
  28.3 0.0 collective-permute-done.3.two_hbm
  28.3 0.1 collective-permute-start.4
  28.4 0.0 copy-done.6
  28.4 0.6 upper_operators.1.ops_ref
  29.0 0.0 copy-start.2
  29.0 0.0 copy-start.7
  29.0 1.7 %collective-permute-start.5 = (bf16[8,2,64,512]{3,2,1,0:T(8,128)(2,1)S(1)}, bf16[8,2,64,512]{3,2,1,0:T(8,128)(2,1)S(1)}, u32[]{:S(2)}, u32[]{:S(2)}) collective-permute-start(bf16[8,2,64,512]{3,2,1,0:T(8,128)(2,1)S(1)} %get-tuple-element.25.own_ref), channel_id=1, source_target_pairs={{0,2},{2,0},{4,6},{6,4},{8,10},{10,8},{12,14},{14,12},{16,18},{18,... | collective-permute-start | bytes 3145736 | tf_op jit(solution)/shard_map/ppermute | solution.py:586
  30.7 1.7 %collective-permute-start.6 = (bf16[8,2,64,512]{3,2,1,0:T(8,128)(2,1)S(1)}, bf16[8,2,64,512]{3,2,1,0:T(8,128)(2,1)}, u32[]{:S(2)}, u32[]{:S(2)}) collective-permute-start(bf16[8,2,64,512]{3,2,1,0:T(8,128)(2,1)S(1)} %get-tuple-element.25.own_ref), channel_id=1, source_target_pairs={{2,4},{4,2},{6,8},{8,6},{10,12},{12,10},{14,16},{16,14},{18,20},{2... | collective-permute-start | bytes 3145736 | tf_op jit(solution)/shard_map/ppermute | solution.py:585
  32.4 0.0 collective-permute-done.2.one2_hbm
  32.4 0.0 collective-permute-done.4.two2_hbm
  32.4 10.0 %near_field.1 = f32[8,2,64,256]{3,2,1,0:T(8,128)} custom-call(s32[8,3]{1,0:T(8,128)S(1)} %broadcast_subtract_fusion.link_ref, s32[2]{0:T(128)S(1)} %pad_add_fusion.place_ref, bf16[8,3,2,256,512]{4,3,2,1,0:T(8,128)(2,1)} %blocks_hbm.1, bf16[8,2,64,512]{3,2,1,0:T(8,128)(2,1)} %own_hbm.1, bf16[4,2,64,512]{3,2,1,0:T(8,128)(2,1)} %collective-permute-done.1.one_hbm, ...), custom_call_target="tpu_custom_call" | custom-call | flops 1073741824 | bytes 1 | tf_op jit(solution)/shard_map/near_field/pallas_call | solution.py:380
  42.4 0.0 all-to-all-done.kids_ref
  42.5 0.0 copy-done.2
  42.5 4.5 %level_two.1.after_ref = bf16[64,2,8,128]{3,2,1,0:T(8,128)(2,1)} custom-call(bf16[8,2,4,32,128]{4,3,2,1,0:T(8,128)(2,1)S(1)} %all-to-all-done.kids_ref, bf16[128,256]{1,0:T(8,128)(2,1)S(1)} %copy-done.2, bf16[64,32]{1,0:T(8,128)(2,1)S(1)} %copy.23.theta_ref, bf16[8,2,64,256]{3,2,1,0:T(8,128)(2,1)S(1)} %reshape.28.shift_ref), custom_call_target="tpu_custom_call" | custom-call | flops 1 | bytes 1 | tf_op jit(solution)/shard_map/level_two/pallas_call | solution.py:224
  47.0 13.2 %all-to-all-start.1 = ((bf16[128,8,128]{2,1,0:T(8,128)(2,1)}), bf16[128,8,128]{2,1,0:T(8,128)(2,1)S(1)}, u32[]{:S(2)}, u32[]{:S(2)}) async-start(bf16[128,8,128]{2,1,0:T(8,128)(2,1)} %bitcast.3), calls=%async_computation.1 | async-start | bytes 524288 | tf_op jit(solution)/shard_map/all_to_all | solution.py:591
  60.2 0.0 copy-done.7
  60.2 0.0 copy-start
  60.2 0.0 copy-start.4
  60.2 0.0 copy-start.5
  60.2 1.0 %copy-done = bf16[316,2,512]{2,1,0:T(2,128)(2,1)S(1)} copy-done((bf16[316,2,512]{2,1,0:T(2,128)(2,1)S(1)}, bf16[316,2,512]{2,1,0:T(2,128)(2,1)}, u32[]{:S(2)}) %copy-start) | copy-done | bytes 647192
  61.3 0.0 copy-done.4
  61.3 0.0 copy-done.5
  61.3 1.3 %leaf_operators.1.ops_ref = f32[8,16,2,512]{3,2,1,0:T(2,128)S(1)} custom-call(s32[8,16]{1,0:T(8,128)S(1)} %copy-done.4, s32[8]{0:T(128)S(1)} %copy-done.5, bf16[316,2,512]{2,1,0:T(2,128)(2,1)S(1)} %copy-done, s32[8,16]{1,0:T(8,128)S(1)} %leaf_links.1.after_ref.link_ref), custom_call_target="tpu_custom_call" | custom-call | flops 1048576 | bytes 1 | tf_op jit(solution)/shard_map/leaf_operators/pallas_call | solution.py:415
  62.6 0.0 collective-permute-done.5.one_ref
  62.6 0.0 collective-permute-done.6.two_ref
  62.6 6.4 %leaf_translate.1 = f32[8,2,64,512]{3,2,1,0:T(8,128)} custom-call(s32[2]{0:T(128)S(1)} %pad_add_fusion.place_ref, s32[8,16]{1,0:T(8,128)S(1)} %leaf_links.1.after_ref.link_ref, s32[8]{0:T(128)S(1)} %copy-done.5, f32[8,16,2,512]{3,2,1,0:T(2,128)S(1)} %leaf_operators.1.ops_ref, bf16[8,2,64,512]{3,2,1,0:T(8,128)(2,1)S(1)} %get-tuple-element.25.own_ref, ...), custom_call_target="tpu_custom_call" | custom-call | flops 1073741824 | bytes 1 | tf_op jit(solution)/shard_map/leaf_translate/pallas_call | solution.py:524
  69.0 2.0 %all-to-all-done.1 = bf16[128,8,128]{2,1,0:T(8,128)(2,1)S(1)} async-done(((bf16[128,8,128]{2,1,0:T(8,128)(2,1)}), bf16[128,8,128]{2,1,0:T(8,128)(2,1)S(1)}, u32[]{:S(2)}, u32[]{:S(2)}) %all-to-all-start.1) | async-done | bytes 262176 | tf_op jit(solution)/shard_map/all_to_all | solution.py:591
  71.1 1.8 %upper_translate.1 = f32[8,2,64,128]{3,2,1,0:T(8,128)} custom-call(s32[8,4]{1,0:T(8,128)S(1)} %copy.24.src_ref, bf16[8,8,2,8,128]{4,3,2,1,0:T(8,128)(2,1)S(1)} %bitcast.9, f32[8,4,2,128]{3,2,1,0:T(2,128)S(1)} %upper_operators.1.ops_ref), custom_call_target="tpu_custom_call" | custom-call | flops 17179869184 | bytes 1 | tf_op jit(solution)/shard_map/upper_translate/pallas_call | solution.py:288
  (2 shorter events, 0.0 us)
Async XLA Ops:
  0.6 11.6 %copy-start.8 = (bf16[8,2,16384]{2,1,0:T(2,128)(2,1)S(1)}, bf16[8,2,16384]{2,1,0:T(2,128)(2,1)}, u32[]{:S(2)}) copy-start(bf16[8,2,16384]{2,1,0:T(2,128)(2,1)} %param.30) | copy-start | bytes 1572868
  0.6 11.9 %copy-start.10 = (bf16[32,16]{0,1:T(8,128)(2,1)S(1)}, bf16[32,16]{0,1:T(8,128)(2,1)}, u32[]{:S(2)}) copy-start(bf16[32,16]{0,1:T(8,128)(2,1)} %param.26) | copy-start | bytes 3076
  0.7 12.0 %copy-start.11 = (s32[8,3]{0,1:T(4,128)S(1)}, s32[8,3]{0,1:T(4,128)}, u32[]{:S(2)}) copy-start(s32[8,3]{0,1:T(4,128)} %param.19) | copy-start | bytes 292
  0.7 12.1 %copy-start.12 = (s32[8,4]{0,1:T(4,128)S(1)}, s32[8,4]{0,1:T(4,128)}, u32[]{:S(2)}) copy-start(s32[8,4]{0,1:T(4,128)} %param.32) | copy-start | bytes 388
  0.7 12.2 %copy-start.9 = (bf16[64,32]{0,1:T(8,128)(2,1)S(1)}, bf16[64,32]{0,1:T(8,128)(2,1)}, u32[]{:S(2)}) copy-start(bf16[64,32]{0,1:T(8,128)(2,1)} %param.29) | copy-start | bytes 12292
  0.7 12.2 %copy-start.13 = (s32[8,4]{0,1:T(4,128)S(1)}, s32[8,4]{0,1:T(4,128)}, u32[]{:S(2)}) copy-start(s32[8,4]{0,1:T(4,128)} %param.31) | copy-start | bytes 388
  0.7 12.4 %copy-start.3 = (bf16[64,128]{1,0:T(8,128)(2,1)S(1)}, bf16[64,128]{1,0:T(8,128)(2,1)}, u32[]{:S(2)}) copy-start(bf16[64,128]{1,0:T(8,128)(2,1)} %phi_ref.2) | copy-start | bytes 49156
  0.7 12.4 %copy-start.1 = (bf16[8,2,4096]{2,1,0:T(2,128)(2,1)S(1)}, bf16[8,2,4096]{2,1,0:T(2,128)(2,1)}, u32[]{:S(2)}) copy-start(bf16[8,2,4096]{2,1,0:T(2,128)(2,1)} %shift_ref.1) | copy-start | bytes 393220
  0.7 27.6 %copy-start.6 = (bf16[316,2,1,128]{3,1,2,0:T(2,128)(2,1)S(1)}, bf16[316,2,1,128]{3,1,2,0:T(2,128)(2,1)}, u32[]{:S(2)}) copy-start(bf16[316,2,1,128]{3,1,2,0:T(2,128)(2,1)} %param.33) | copy-start | bytes 485380
  7.5 5.6 %collective-permute-start = (bf16[8,2,32,512]{3,2,1,0:T(8,128)(2,1)}, bf16[8,2,32,512]{3,2,1,0:T(8,128)(2,1)S(1)}, u32[]{:S(2)}, u32[]{:S(2)}) collective-permute-start(bf16[8,2,32,512]{3,2,1,0:T(8,128)(2,1)} %get-tuple-element.18), channel_id=1, source_target_pairs={{0,1},{1,0},{2,3},{3,2},{4,5},{5,4},{6,7},{7,6},{8,9},{9,8},{10,11... | collective-permute-start | bytes 1572872 | tf_op jit(solution)/shard_map/ppermute | solution.py:572
  9.0 18.2 %collective-permute-start.1 = (bf16[4,2,64,512]{3,2,1,0:T(8,128)(2,1)}, bf16[4,2,64,512]{3,2,1,0:T(8,128)(2,1)}, u32[]{:S(2)}, u32[]{:S(2)}) collective-permute-start(bf16[4,2,64,512]{3,2,1,0:T(8,128)(2,1)} %get-tuple-element.21), channel_id=1, source_target_pairs={{0,2},{2,0},{4,6},{6,4},{8,10},{10,8},{12,14},{14,12},{16,18},{18,... | collective-permute-start | bytes 1572872 | tf_op jit(solution)/shard_map/ppermute | solution.py:574
  10.8 17.5 %collective-permute-start.3 = (bf16[4,2,64,512]{3,2,1,0:T(8,128)(2,1)}, bf16[4,2,64,512]{3,2,1,0:T(8,128)(2,1)}, u32[]{:S(2)}, u32[]{:S(2)}) collective-permute-start(bf16[4,2,64,512]{3,2,1,0:T(8,128)(2,1)} %get-tuple-element.21), channel_id=1, source_target_pairs={{2,4},{4,2},{6,8},{8,6},{10,12},{12,10},{14,16},{16,14},{18,20},{2... | collective-permute-start | bytes 1572872 | tf_op jit(solution)/shard_map/ppermute | solution.py:573
  21.0 21.5 %all-to-all-start = ((bf16[8,2,4,32,128]{4,3,2,1,0:T(8,128)(2,1)}), bf16[8,2,4,32,128]{4,3,2,1,0:T(8,128)(2,1)S(1)}, u32[]{:S(2)}, u32[]{:S(2)}) async-start(bf16[8,2,4,32,128]{4,3,2,1,0:T(8,128)(2,1)} %level_one.1.after_ref), calls=%async_computation | async-start | bytes 1048576 | tf_op jit(solution)/shard_map/all_to_all | solution.py:580
  27.3 5.2 %collective-permute-start.2 = (bf16[4,2,64,512]{3,2,1,0:T(8,128)(2,1)}, bf16[4,2,64,512]{3,2,1,0:T(8,128)(2,1)S(1)}, u32[]{:S(2)}, u32[]{:S(2)}) collective-permute-start(bf16[4,2,64,512]{3,2,1,0:T(8,128)(2,1)} %collective-permute-done.1.one_hbm), channel_id=1, source_target_pairs={{0,1},{1,0},{2,3},{3,2},{4,5},{5,4},{6,7},{7,6},{8,9},{9,8},{10,11... | collective-permute-start | bytes 1572872 | tf_op jit(solution)/shard_map/ppermute | solution.py:576
  28.3 4.2 %collective-permute-start.4 = (bf16[4,2,64,512]{3,2,1,0:T(8,128)(2,1)}, bf16[4,2,64,512]{3,2,1,0:T(8,128)(2,1)S(1)}, u32[]{:S(2)}, u32[]{:S(2)}) collective-permute-start(bf16[4,2,64,512]{3,2,1,0:T(8,128)(2,1)} %collective-permute-done.3.two_hbm), channel_id=1, source_target_pairs={{0,1},{1,0},{2,3},{3,2},{4,5},{5,4},{6,7},{7,6},{8,9},{9,8},{10,11... | collective-permute-start | bytes 1572872 | tf_op jit(solution)/shard_map/ppermute | solution.py:575
  29.0 13.5 %copy-start.2 = (bf16[128,256]{1,0:T(8,128)(2,1)S(1)}, bf16[128,256]{1,0:T(8,128)(2,1)}, u32[]{:S(2)}) copy-start(bf16[128,256]{1,0:T(8,128)(2,1)} %phi_ref.3) | copy-start | bytes 196612
  29.0 31.2 %copy-start.7 = (s32[8,16]{1,0:T(8,128)S(1)}, s32[8,16]{1,0:T(8,128)}, u32[]{:S(2)}) copy-start(s32[8,16]{1,0:T(8,128)} %src_ref.2) | copy-start | bytes 1540
  29.0 33.6 %collective-permute-start.5 = (bf16[8,2,64,512]{3,2,1,0:T(8,128)(2,1)S(1)}, bf16[8,2,64,512]{3,2,1,0:T(8,128)(2,1)S(1)}, u32[]{:S(2)}, u32[]{:S(2)}) collective-permute-start(bf16[8,2,64,512]{3,2,1,0:T(8,128)(2,1)S(1)} %get-tuple-element.25.own_ref), channel_id=1, source_target_pairs={{0,2},{2,0},{4,6},{6,4},{8,10},{10,8},{12,14},{14,12},{16,18},{18,... | collective-permute-start | bytes 3145736 | tf_op jit(solution)/shard_map/ppermute | solution.py:586
  30.7 31.8 %collective-permute-start.6 = (bf16[8,2,64,512]{3,2,1,0:T(8,128)(2,1)S(1)}, bf16[8,2,64,512]{3,2,1,0:T(8,128)(2,1)}, u32[]{:S(2)}, u32[]{:S(2)}) collective-permute-start(bf16[8,2,64,512]{3,2,1,0:T(8,128)(2,1)S(1)} %get-tuple-element.25.own_ref), channel_id=1, source_target_pairs={{2,4},{4,2},{6,8},{8,6},{10,12},{12,10},{14,16},{16,14},{18,20},{2... | collective-permute-start | bytes 3145736 | tf_op jit(solution)/shard_map/ppermute | solution.py:585
  47.0 24.1 %all-to-all-start.1 = ((bf16[128,8,128]{2,1,0:T(8,128)(2,1)}), bf16[128,8,128]{2,1,0:T(8,128)(2,1)S(1)}, u32[]{:S(2)}, u32[]{:S(2)}) async-start(bf16[128,8,128]{2,1,0:T(8,128)(2,1)} %bitcast.3), calls=%async_computation.1 | async-start | bytes 524288 | tf_op jit(solution)/shard_map/all_to_all | solution.py:591
  60.2 1.1 %copy-start = (bf16[316,2,512]{2,1,0:T(2,128)(2,1)S(1)}, bf16[316,2,512]{2,1,0:T(2,128)(2,1)}, u32[]{:S(2)}) copy-start(bf16[316,2,512]{2,1,0:T(2,128)(2,1)} %ops_ref.1) | copy-start | bytes 1941508
  60.2 1.1 %copy-start.4 = (s32[8,16]{1,0:T(8,128)S(1)}, s32[8,16]{1,0:T(8,128)}, u32[]{:S(2)}) copy-start(s32[8,16]{1,0:T(8,128)} %rel_ref.2) | copy-start | bytes 1540
  60.2 1.1 %copy-start.5 = (s32[8]{0:T(128)S(1)}, s32[8]{0:T(128)}, u32[]{:S(2)}) copy-start(s32[8]{0:T(128)} %count_ref.3) | copy-start | bytes 100

commit v4 on v3

--- a/solution.py
+++ b/solution.py
@@ -394,7 +394,7 @@
         compiler_params=params(24),
         cost_estimate=cost(1 << 30, 1),
         name="near_field",
-    )(links, places, in_hbm(near_blocks), in_hbm(own), one, one2, two, two2)
+    )(links, places, near_blocks, in_hbm(own), one, one2, two, two2)
 
 
 def gather_kernel(rel_ref, count_ref, ops_ref, after_ref, out_ref):
@@ -402,10 +402,14 @@
 
     def box(b, carry):
         def entry(i, inner):
-            out_ref[b, i] = ops_ref[rel_ref[b, i]].astype(F32)
+            row = ops_ref[rel_ref[b, i]].astype(F32)
+            out_ref[b, i, 0] = jnp.broadcast_to(row[0:1], (16, 512)).astype(BF16)
+            out_ref[b, i, 1] = jnp.broadcast_to(row[1:2], (16, 512)).astype(BF16)
             return inner
 
-        lax.fori_loop(0, count_ref[b], entry, 0)
+        count = count_ref[b]
+        lax.fori_loop(0, count, entry, 0)
+        out_ref[b, count] = jnp.zeros((2, 16, 512), BF16)
         return carry
 
     lax.fori_loop(0, 8, box, 0)
@@ -416,8 +420,8 @@
         gather_kernel,
         in_specs=[SMEM, SMEM, VMEM, ANYWHERE],
         out_specs=VMEM,
-        out_shape=jax.ShapeDtypeStruct((8, 16, 2, 512), F32),
-        compiler_params=params(8),
+        out_shape=jax.ShapeDtypeStruct((8, 17, 2, 16, 512), BF16),
+        compiler_params=params(12),
         cost_estimate=cost(1 << 20, 1),
         name="leaf_operators",
     )(rel, count, operators, after)
@@ -450,7 +454,6 @@
     two_ref,
     out_hbm,
     boxes,
-    wide,
     result,
     box_sems,
     out_sems,
@@ -471,15 +474,6 @@
     def box(b, carry):
         count = count_ref[b]
 
-        def widen(i, inner):
-            row = ops_ref[b, i]
-            wide[i, 0] = jnp.broadcast_to(row[0:1], (16, 512)).astype(BF16)
-            wide[i, 1] = jnp.broadcast_to(row[1:2], (16, 512)).astype(BF16)
-            return inner
-
-        lax.fori_loop(0, count, widen, 0)
-        wide[count] = jnp.zeros((2, 16, 512), BF16)
-
         @pl.when(b == 0)
         def _():
             for copy in copies:
@@ -493,8 +487,8 @@
                 link = link_ref[b, jnp.minimum(i, 15)]
                 real_part = boxes[link, 0, chunk, :].reshape(size // 16, 16, 512)
                 imag_part = boxes[link, 1, chunk, :].reshape(size // 16, 16, 512)
-                op_real = wide[i, 0][None]
-                op_imag = wide[i, 1][None]
+                op_real = ops_ref[b, i, 0][None]
+                op_imag = ops_ref[b, i, 1][None]
                 return (
                     op_real * real_part - op_imag * imag_part,
                     op_real * imag_part + op_imag * real_part,
@@ -528,7 +522,6 @@
         out_shape=jax.ShapeDtypeStruct((8, 2, 64, 512), F32),
         scratch_shapes=[
             pltpu.VMEM((24, 2, 64, 512), BF16),
-            pltpu.VMEM((18, 2, 16, 512), BF16),
             pltpu.VMEM((8, 2, 64, 512), F32),
             pltpu.SemaphoreType.DMA((3,)),
             pltpu.SemaphoreType.DMA((8,)),

time: 74.3 us -> 74.3 us (level)
  the two profiles are of different devices: /device:TPU:1 before, /device:TPU:118 now
where the time goes in v4:
time: 74.3 us; the launch traced here: 73.5 us
  Pallas kernels  38.3 us (52%)
  starting transfers between devices  22 us (30%)
  waiting for transfers between devices  9.44 us (13%)
  local copies, waits for them, and re-layouts  2.73 us (4%)
  between operations  1.01 us (1%)
    all_to_all x1, starting transfers between devices, local(): got = lax.all_to_all(terms.reshape(128, 8, 128), ALL, 0, 0, tiled=True)  9.57 us
    pallas_call x1, Pallas kernels, near_products(): pl.pallas_call(near_kernel, in_specs=[SMEM, SMEM] + [HBM] * 6, out_specs=...  9.07 us
    pallas_call x1, Pallas kernels, level_one_patterns(): pl.pallas_call(level_one_kernel, grid_spec=pltpu.PrefetchScalarGridSpec(n...  7.85 us
    pallas_call x1, Pallas kernels, leaf_patterns(): pl.pallas_call(leaf_kernel, in_specs=[SMEM, HBM, HBM], out_specs=[HBM, HB...  6.79 us
    pallas_call x1, Pallas kernels, leaf_translate(): pl.pallas_call(translate_kernel, in_specs=[SMEM] * 3 + [VMEM] + [ANYWHERE...  6 us
    all_to_all x1, starting transfers between devices, local(): kids = lax.all_to_all(level_one, ('xl', 'z'), 0, 0, tiled=True)  5.55 us
    ppermute x1, waiting for transfers between devices, local(): leaf_two = lax.ppermute(leaf, BOX, with_two)  4.88 us
    ppermute x1, waiting for transfers between devices, local(): two = lax.ppermute(half, BOX, with_two)  4.55 us
  transfers between devices with their start and end apart: 9, of which 2 were waited for; matrix products, arithmetic and copies ran while one was open for 1% of the time, Pallas kernels for 40%

profile of v4, /device:TPU:118, one launch (start us, length us, event | category | flops | bytes accessed | tf_op | source)
XLA Modules:
  0.0 73.5 jit_solution(182831391084700949)
XLA Ops:
  0.6 0.0 copy-start.8
  0.6 0.0 copy-start.10
  0.7 0.0 copy-start.11
  0.7 0.0 copy-start.12
  0.7 0.0 copy-start.9
  0.7 0.0 copy-start.13
  0.7 0.0 copy-start.3
  0.7 0.0 copy-start.1
  0.7 0.0 copy-start.6
  0.7 6.8 %leaf_patterns.1 = (bf16[4,2,64,512]{3,2,1,0:T(8,128)(2,1)}, bf16[8,2,32,512]{3,2,1,0:T(8,128)(2,1)}, bf16[8,2,64,512]{3,2,1,0:T(8,128)(2,1)S(1)}, bf16[8,2,32,512]{3,2,1,0:T(8,128)(2,1)S(1)}) custom-call(s32[1]{0:T(128)} %bitcast.dir_ref, bf16[8,2,64,512]{3,2,1,0:T(8,128)(2,1)} %own_hbm.1, bf16[8,2,512,512]{3,2,1,0:T(8,128)(2,1)} %rad_hbm.1), custom_call_target="tpu_custom_call" | custom-call | flops 1 | bytes 1 | tf_op jit(solution)/shard_map/leaf_patterns/pallas_call | solution.py:86
  7.5 0.1 collective-permute-start
  7.6 0.5 collective-permute-start.1
  8.1 3.2 %collective-permute-start.3 = (bf16[4,2,64,512]{3,2,1,0:T(8,128)(2,1)}, bf16[4,2,64,512]{3,2,1,0:T(8,128)(2,1)}, u32[]{:S(2)}, u32[]{:S(2)}) collective-permute-start(bf16[4,2,64,512]{3,2,1,0:T(8,128)(2,1)} %get-tuple-element.21), channel_id=1, source_target_pairs={{2,4},{4,2},{6,8},{8,6},{10,12},{12,10},{14,16},{16,14},{18,20},{2... | collective-permute-start | bytes 1572872 | tf_op jit(solution)/shard_map/ppermute | solution.py:566
  11.4 0.0 copy-done.8
  11.4 0.3 reshape.28.shift_ref
  11.7 0.0 copy-done.10
  11.7 0.1 copy.20.theta_ref
  11.8 0.0 copy-done.11
  11.8 0.1 copy.21
  11.9 0.0 copy-done.12
  11.9 0.1 copy.22.rel_ref
  12.0 0.0 copy-done.9
  12.0 0.1 copy.23.theta_ref
  12.1 0.0 copy-done.13
  12.1 0.1 copy.24.src_ref
  12.2 0.1 pad_add_fusion.place_ref
  12.3 0.0 collective-permute-done.other_ref
  12.3 0.0 copy-done.3
  12.3 0.0 copy-done.1
  12.3 7.9 %level_one.1.after_ref = bf16[8,2,4,32,128]{4,3,2,1,0:T(8,128)(2,1)} custom-call(s32[1]{0:T(128)} %bitcast.dir_ref, bf16[8,2,32,512]{3,2,1,0:T(8,128)(2,1)S(1)} %get-tuple-element.17.mine_ref, bf16[8,2,32,512]{3,2,1,0:T(8,128)(2,1)S(1)} %collective-permute-done.other_ref, bf16[64,128]{1,0:T(8,128)(2,1)S(1)} %copy-done.3, bf16[32,16]{1,0:T(8,128)(2,1)S(1)} %copy.20.theta_ref, ...), custom_call_target="tpu_custom_call" | custom-call | flops 1 | bytes 1 | tf_op jit(solution)/shard_map/level_one/pallas_call | solution.py:163
  20.1 5.5 %all-to-all-start = ((bf16[8,2,4,32,128]{4,3,2,1,0:T(8,128)(2,1)}), bf16[8,2,4,32,128]{4,3,2,1,0:T(8,128)(2,1)S(1)}, u32[]{:S(2)}, u32[]{:S(2)}) async-start(bf16[8,2,4,32,128]{4,3,2,1,0:T(8,128)(2,1)} %level_one.1.after_ref), calls=%async_computation | async-start | bytes 1048576 | tf_op jit(solution)/shard_map/all_to_all | solution.py:573
  25.7 0.0 collective-permute-done.1.one_hbm
  25.7 0.0 collective-permute-start.2
  25.7 4.5 %collective-permute-done.3.two_hbm = bf16[4,2,64,512]{3,2,1,0:T(8,128)(2,1)} collective-permute-done((bf16[4,2,64,512]{3,2,1,0:T(8,128)(2,1)}, bf16[4,2,64,512]{3,2,1,0:T(8,128)(2,1)}, u32[]{:S(2)}, u32[]{:S(2)}) %collective-permute-start.3) | collective-permute-done | bytes 524320 | tf_op jit(solution)/shard_map/ppermute | solution.py:566
  30.2 0.0 collective-permute-start.4
  30.2 0.0 copy-done.6
  30.3 0.0 slice-start.1
  30.3 0.0 slice-start.2
  30.3 0.6 upper_operators.1.ops_ref
  30.9 0.0 copy-start.2
  30.9 0.0 copy-start.7
  30.9 0.1 collective-permute-start.5
  31.0 3.0 %collective-permute-start.6 = (bf16[8,2,64,512]{3,2,1,0:T(8,128)(2,1)S(1)}, bf16[8,2,64,512]{3,2,1,0:T(8,128)(2,1)}, u32[]{:S(2)}, u32[]{:S(2)}) collective-permute-start(bf16[8,2,64,512]{3,2,1,0:T(8,128)(2,1)S(1)} %get-tuple-element.25.own_ref), channel_id=1, source_target_pairs={{2,4},{4,2},{6,8},{8,6},{10,12},{12,10},{14,16},{16,14},{18,20},{2... | collective-permute-start | bytes 3145736 | tf_op jit(solution)/shard_map/ppermute | solution.py:578
  34.0 0.0 collective-permute-done.2.one2_hbm
  34.0 0.0 collective-permute-done.4.two2_hbm
  34.0 0.0 slice-done
  34.0 0.0 slice-done.1
  34.1 0.9 %slice-done.2 = s8[4194304]{0:T(1024)(128)(4,1)S(1)} async-done(((s8[12582912]{0:T(1024)(128)(4,1)}), s8[4194304]{0:T(1024)(128)(4,1)S(1)}, s32[]{:S(2)}) %slice-start.2) | async-done | bytes 4194328
  34.9 9.1 %near_field.1 = f32[8,2,64,256]{3,2,1,0:T(8,128)} custom-call(s32[8,3]{1,0:T(8,128)S(1)} %broadcast_subtract_fusion.link_ref, s32[2]{0:T(128)S(1)} %pad_add_fusion.place_ref, bf16[8,3,2,256,512]{4,3,2,1,0:T(8,128)(2,1)S(1)} %bitcast.10, bf16[8,2,64,512]{3,2,1,0:T(8,128)(2,1)} %own_hbm.1, bf16[4,2,64,512]{3,2,1,0:T(8,128)(2,1)} %collective-permute-done.1.one_hbm, ...), custom_call_target="tpu_custom_call" | custom-call | flops 1073741824 | bytes 1 | tf_op jit(solution)/shard_map/near_field/pallas_call | solution.py:380
  44.0 0.0 all-to-all-done.kids_ref
  44.0 0.0 copy-done.2
  44.0 4.5 %level_two.1.after_ref = bf16[64,2,8,128]{3,2,1,0:T(8,128)(2,1)} custom-call(bf16[8,2,4,32,128]{4,3,2,1,0:T(8,128)(2,1)S(1)} %all-to-all-done.kids_ref, bf16[128,256]{1,0:T(8,128)(2,1)S(1)} %copy-done.2, bf16[64,32]{1,0:T(8,128)(2,1)S(1)} %copy.23.theta_ref, bf16[8,2,64,256]{3,2,1,0:T(8,128)(2,1)S(1)} %reshape.28.shift_ref), custom_call_target="tpu_custom_call" | custom-call | flops 1 | bytes 1 | tf_op jit(solution)/shard_map/level_two/pallas_call | solution.py:224
  48.5 9.6 %all-to-all-start.1 = ((bf16[128,8,128]{2,1,0:T(8,128)(2,1)}), bf16[128,8,128]{2,1,0:T(8,128)(2,1)S(1)}, u32[]{:S(2)}, u32[]{:S(2)}) async-start(bf16[128,8,128]{2,1,0:T(8,128)(2,1)} %bitcast.3), calls=%async_computation.1 | async-start | bytes 524288 | tf_op jit(solution)/shard_map/all_to_all | solution.py:584
  58.1 0.0 copy-start
  58.1 0.0 copy-start.4
  58.1 0.0 copy-start.5
  58.1 1.0 %copy-done = bf16[316,2,512]{2,1,0:T(2,128)(2,1)S(1)} copy-done((bf16[316,2,512]{2,1,0:T(2,128)(2,1)S(1)}, bf16[316,2,512]{2,1,0:T(2,128)(2,1)}, u32[]{:S(2)}) %copy-start) | copy-done | bytes 647192
  59.2 0.0 copy-done.4
  59.2 1.6 %leaf_operators.1.ops_ref = bf16[8,17,2,16,512]{4,3,2,1,0:T(8,128)(2,1)S(1)} custom-call(s32[8,16]{1,0:T(8,128)S(1)} %copy-done.4, s32[8]{0:T(128)S(1)} %copy-done.5, bf16[316,2,512]{2,1,0:T(2,128)(2,1)S(1)} %copy-done, s32[8,16]{1,0:T(8,128)S(1)} %leaf_links.1.after_ref.link_ref), custom_call_target="tpu_custom_call" | custom-call | flops 1048576 | bytes 1 | tf_op jit(solution)/shard_map/leaf_operators/pallas_call | solution.py:419
  60.8 0.0 collective-permute-done.5.one_ref
  60.8 4.9 %collective-permute-done.6.two_ref = bf16[8,2,64,512]{3,2,1,0:T(8,128)(2,1)} collective-permute-done((bf16[8,2,64,512]{3,2,1,0:T(8,128)(2,1)S(1)}, bf16[8,2,64,512]{3,2,1,0:T(8,128)(2,1)}, u32[]{:S(2)}, u32[]{:S(2)}) %collective-permute-start.6) | collective-permute-done | bytes 1048608 | tf_op jit(solution)/shard_map/ppermute | solution.py:578
  65.7 6.0 %leaf_translate.1 = f32[8,2,64,512]{3,2,1,0:T(8,128)} custom-call(s32[2]{0:T(128)S(1)} %pad_add_fusion.place_ref, s32[8,16]{1,0:T(8,128)S(1)} %leaf_links.1.after_ref.link_ref, s32[8]{0:T(128)S(1)} %copy-done.5, bf16[8,17,2,16,512]{4,3,2,1,0:T(8,128)(2,1)S(1)} %leaf_operators.1.ops_ref, bf16[8,2,64,512]{3,2,1,0:T(8,128)(2,1)S(1)} %get-tuple-element.25.own_ref, ...), custom_call_target="tpu_custom_call" | custom-call | flops 1073741824 | bytes 1 | tf_op jit(solution)/shard_map/leaf_translate/pallas_call | solution.py:518
  71.7 0.0 all-to-all-done.1
  71.7 1.8 %upper_translate.1 = f32[8,2,64,128]{3,2,1,0:T(8,128)} custom-call(s32[8,4]{1,0:T(8,128)S(1)} %copy.24.src_ref, bf16[8,8,2,8,128]{4,3,2,1,0:T(8,128)(2,1)S(1)} %bitcast.11, f32[8,4,2,128]{3,2,1,0:T(2,128)S(1)} %upper_operators.1.ops_ref), custom_call_target="tpu_custom_call" | custom-call | flops 17179869184 | bytes 1 | tf_op jit(solution)/shard_map/upper_translate/pallas_call | solution.py:288
  (6 shorter events, 0.0 us)
Async XLA Ops:
  0.6 10.7 %copy-start.8 = (bf16[8,2,16384]{2,1,0:T(2,128)(2,1)S(1)}, bf16[8,2,16384]{2,1,0:T(2,128)(2,1)}, u32[]{:S(2)}) copy-start(bf16[8,2,16384]{2,1,0:T(2,128)(2,1)} %param.30) | copy-start | bytes 1572868
  0.6 11.1 %copy-start.10 = (bf16[32,16]{0,1:T(8,128)(2,1)S(1)}, bf16[32,16]{0,1:T(8,128)(2,1)}, u32[]{:S(2)}) copy-start(bf16[32,16]{0,1:T(8,128)(2,1)} %param.26) | copy-start | bytes 3076
  0.7 11.2 %copy-start.11 = (s32[8,3]{0,1:T(4,128)S(1)}, s32[8,3]{0,1:T(4,128)}, u32[]{:S(2)}) copy-start(s32[8,3]{0,1:T(4,128)} %param.19) | copy-start | bytes 292
  0.7 11.2 %copy-start.12 = (s32[8,4]{0,1:T(4,128)S(1)}, s32[8,4]{0,1:T(4,128)}, u32[]{:S(2)}) copy-start(s32[8,4]{0,1:T(4,128)} %param.32) | copy-start | bytes 388
  0.7 11.3 %copy-start.9 = (bf16[64,32]{0,1:T(8,128)(2,1)S(1)}, bf16[64,32]{0,1:T(8,128)(2,1)}, u32[]{:S(2)}) copy-start(bf16[64,32]{0,1:T(8,128)(2,1)} %param.29) | copy-start | bytes 12292
  0.7 11.4 %copy-start.13 = (s32[8,4]{0,1:T(4,128)S(1)}, s32[8,4]{0,1:T(4,128)}, u32[]{:S(2)}) copy-start(s32[8,4]{0,1:T(4,128)} %param.31) | copy-start | bytes 388
  0.7 11.6 %copy-start.3 = (bf16[64,128]{1,0:T(8,128)(2,1)S(1)}, bf16[64,128]{1,0:T(8,128)(2,1)}, u32[]{:S(2)}) copy-start(bf16[64,128]{1,0:T(8,128)(2,1)} %phi_ref.2) | copy-start | bytes 49156
  0.7 11.6 %copy-start.1 = (bf16[8,2,4096]{2,1,0:T(2,128)(2,1)S(1)}, bf16[8,2,4096]{2,1,0:T(2,128)(2,1)}, u32[]{:S(2)}) copy-start(bf16[8,2,4096]{2,1,0:T(2,128)(2,1)} %shift_ref.1) | copy-start | bytes 393220
  0.7 29.5 %copy-start.6 = (bf16[316,2,1,128]{3,1,2,0:T(2,128)(2,1)S(1)}, bf16[316,2,1,128]{3,1,2,0:T(2,128)(2,1)}, u32[]{:S(2)}) copy-start(bf16[316,2,1,128]{3,1,2,0:T(2,128)(2,1)} %param.33) | copy-start | bytes 485380
  7.5 4.7 %collective-permute-start = (bf16[8,2,32,512]{3,2,1,0:T(8,128)(2,1)}, bf16[8,2,32,512]{3,2,1,0:T(8,128)(2,1)S(1)}, u32[]{:S(2)}, u32[]{:S(2)}) collective-permute-start(bf16[8,2,32,512]{3,2,1,0:T(8,128)(2,1)} %get-tuple-element.18), channel_id=1, source_target_pairs={{0,1},{1,0},{2,3},{3,2},{4,5},{5,4},{6,7},{7,6},{8,9},{9,8},{10,11... | collective-permute-start | bytes 1572872 | tf_op jit(solution)/shard_map/ppermute | solution.py:565
  7.6 18.1 %collective-permute-start.1 = (bf16[4,2,64,512]{3,2,1,0:T(8,128)(2,1)}, bf16[4,2,64,512]{3,2,1,0:T(8,128)(2,1)}, u32[]{:S(2)}, u32[]{:S(2)}) collective-permute-start(bf16[4,2,64,512]{3,2,1,0:T(8,128)(2,1)} %get-tuple-element.21), channel_id=1, source_target_pairs={{0,2},{2,0},{4,6},{6,4},{8,10},{10,8},{12,14},{14,12},{16,18},{18,... | collective-permute-start | bytes 1572872 | tf_op jit(solution)/shard_map/ppermute | solution.py:567
  8.1 22.1 %collective-permute-start.3 = (bf16[4,2,64,512]{3,2,1,0:T(8,128)(2,1)}, bf16[4,2,64,512]{3,2,1,0:T(8,128)(2,1)}, u32[]{:S(2)}, u32[]{:S(2)}) collective-permute-start(bf16[4,2,64,512]{3,2,1,0:T(8,128)(2,1)} %get-tuple-element.21), channel_id=1, source_target_pairs={{2,4},{4,2},{6,8},{8,6},{10,12},{12,10},{14,16},{16,14},{18,20},{2... | collective-permute-start | bytes 1572872 | tf_op jit(solution)/shard_map/ppermute | solution.py:566
  20.1 23.9 %all-to-all-start = ((bf16[8,2,4,32,128]{4,3,2,1,0:T(8,128)(2,1)}), bf16[8,2,4,32,128]{4,3,2,1,0:T(8,128)(2,1)S(1)}, u32[]{:S(2)}, u32[]{:S(2)}) async-start(bf16[8,2,4,32,128]{4,3,2,1,0:T(8,128)(2,1)} %level_one.1.after_ref), calls=%async_computation | async-start | bytes 1048576 | tf_op jit(solution)/shard_map/all_to_all | solution.py:573
  25.7 8.3 %collective-permute-start.2 = (bf16[4,2,64,512]{3,2,1,0:T(8,128)(2,1)}, bf16[4,2,64,512]{3,2,1,0:T(8,128)(2,1)S(1)}, u32[]{:S(2)}, u32[]{:S(2)}) collective-permute-start(bf16[4,2,64,512]{3,2,1,0:T(8,128)(2,1)} %collective-permute-done.1.one_hbm), channel_id=1, source_target_pairs={{0,1},{1,0},{2,3},{3,2},{4,5},{5,4},{6,7},{7,6},{8,9},{9,8},{10,11... | collective-permute-start | bytes 1572872 | tf_op jit(solution)/shard_map/ppermute | solution.py:569
  30.2 3.8 %collective-permute-start.4 = (bf16[4,2,64,512]{3,2,1,0:T(8,128)(2,1)}, bf16[4,2,64,512]{3,2,1,0:T(8,128)(2,1)S(1)}, u32[]{:S(2)}, u32[]{:S(2)}) collective-permute-start(bf16[4,2,64,512]{3,2,1,0:T(8,128)(2,1)} %collective-permute-done.3.two_hbm), channel_id=1, source_target_pairs={{0,1},{1,0},{2,3},{3,2},{4,5},{5,4},{6,7},{7,6},{8,9},{9,8},{10,11... | collective-permute-start | bytes 1572872 | tf_op jit(solution)/shard_map/ppermute | solution.py:568
  30.2 3.8 %slice-start = ((s8[12582912]{0:T(1024)(128)(4,1)}), s8[4194304]{0:T(1024)(128)(4,1)S(1)}, s32[]{:S(2)}) async-start(s8[12582912]{0:T(1024)(128)(4,1)} %bitcast.9), calls=%async_computation.2 | async-start | bytes 8388608
  30.3 3.8 %slice-start.1 = ((s8[12582912]{0:T(1024)(128)(4,1)}), s8[4194304]{0:T(1024)(128)(4,1)S(1)}, s32[]{:S(2)}) async-start(s8[12582912]{0:T(1024)(128)(4,1)} %bitcast.9), calls=%async_computation.3 | async-start | bytes 8388608
  30.3 4.6 %slice-start.2 = ((s8[12582912]{0:T(1024)(128)(4,1)}), s8[4194304]{0:T(1024)(128)(4,1)S(1)}, s32[]{:S(2)}) async-start(s8[12582912]{0:T(1024)(128)(4,1)} %bitcast.9), calls=%async_computation.4 | async-start | bytes 8388608
  30.9 13.1 %copy-start.2 = (bf16[128,256]{1,0:T(8,128)(2,1)S(1)}, bf16[128,256]{1,0:T(8,128)(2,1)}, u32[]{:S(2)}) copy-start(bf16[128,256]{1,0:T(8,128)(2,1)} %phi_ref.3) | copy-start | bytes 196612
  30.9 27.2 %copy-start.7 = (s32[8,16]{1,0:T(8,128)S(1)}, s32[8,16]{1,0:T(8,128)}, u32[]{:S(2)}) copy-start(s32[8,16]{1,0:T(8,128)} %src_ref.2) | copy-start | bytes 1540
  30.9 29.9 %collective-permute-start.5 = (bf16[8,2,64,512]{3,2,1,0:T(8,128)(2,1)S(1)}, bf16[8,2,64,512]{3,2,1,0:T(8,128)(2,1)S(1)}, u32[]{:S(2)}, u32[]{:S(2)}) collective-permute-start(bf16[8,2,64,512]{3,2,1,0:T(8,128)(2,1)S(1)} %get-tuple-element.25.own_ref), channel_id=1, source_target_pairs={{0,2},{2,0},{4,6},{6,4},{8,10},{10,8},{12,14},{14,12},{16,18},{18,... | collective-permute-start | bytes 3145736 | tf_op jit(solution)/shard_map/ppermute | solution.py:579
  31.0 34.7 %collective-permute-start.6 = (bf16[8,2,64,512]{3,2,1,0:T(8,128)(2,1)S(1)}, bf16[8,2,64,512]{3,2,1,0:T(8,128)(2,1)}, u32[]{:S(2)}, u32[]{:S(2)}) collective-permute-start(bf16[8,2,64,512]{3,2,1,0:T(8,128)(2,1)S(1)} %get-tuple-element.25.own_ref), channel_id=1, source_target_pairs={{2,4},{4,2},{6,8},{8,6},{10,12},{12,10},{14,16},{16,14},{18,20},{2... | collective-permute-start | bytes 3145736 | tf_op jit(solution)/shard_map/ppermute | solution.py:578
  48.5 23.2 %all-to-all-start.1 = ((bf16[128,8,128]{2,1,0:T(8,128)(2,1)}), bf16[128,8,128]{2,1,0:T(8,128)(2,1)S(1)}, u32[]{:S(2)}, u32[]{:S(2)}) async-start(bf16[128,8,128]{2,1,0:T(8,128)(2,1)} %bitcast.3), calls=%async_computation.1 | async-start | bytes 524288 | tf_op jit(solution)/shard_map/all_to_all | solution.py:584
  58.1 1.1 %copy-start = (bf16[316,2,512]{2,1,0:T(2,128)(2,1)S(1)}, bf16[316,2,512]{2,1,0:T(2,128)(2,1)}, u32[]{:S(2)}) copy-start(bf16[316,2,512]{2,1,0:T(2,128)(2,1)} %ops_ref.1) | copy-start | bytes 1941508
  58.1 1.1 %copy-start.4 = (s32[8,16]{1,0:T(8,128)S(1)}, s32[8,16]{1,0:T(8,128)}, u32[]{:S(2)}) copy-start(s32[8,16]{1,0:T(8,128)} %rel_ref.2) | copy-start | bytes 1540
  58.1 1.1 %copy-start.5 = (s32[8]{0:T(128)S(1)}, s32[8]{0:T(128)}, u32[]{:S(2)}) copy-start(s32[8]{0:T(128)} %count_ref.3) | copy-start | bytes 100
